TPU v7x, 256 devices: a whole 4x4x8 slice. The times are simulated.
256 devices in a mesh: head: 8 (over y_lo, x), tok: 32 (over z, y_hi, core).
Axes of the slice: x: 4, y: 4 (y_hi: 2, y_lo: 2; y = y_hi * 2 + y_lo), z: 8, core: 2. Of those that a mesh axis runs over, the one named last changes fastest.
Arguments:
- queries: bfloat16 [16384, 5120], P(('tok', 'head')), may hold values from -72 to 72, as said below
- keys_in: bfloat16 [16384, 5120], P(('tok', 'head')), may hold values from -12 to 12, as said below
- values: bfloat16 [16384, 5120], P(('tok', 'head')), may hold values from -8 to 8, as said below
- grad_out: bfloat16 [16384, 5120], P(('tok', 'head')), may hold values from -192 to 192
- fine_gate: bfloat16 [16384, 40], P(('tok', 'head')), may hold values from 0.25 to 1
- coarse_gate: bfloat16 [16384, 40], P(('tok', 'head')), may hold values from 0.25 to 1
- tile_of_cube: int32 [256], replicated, may hold values from 0 to 255, as said below
- select: int32 [256, 16], replicated, may hold values from 0 to 255, as said below
Outputs:
- grad_queries: bfloat16 [16384, 5120], P(('tok', 'head'))
- grad_keys: bfloat16 [16384, 5120], P(('tok', 'head'))
- grad_values: bfloat16 [16384, 5120], P(('tok', 'head'))
Inputs may be any that keep to these rules, and one draw needn't show every extreme that they name: `tile_of_cube`: A permutation: every cube has its own tile. `select`: each row lists 16 distinct cubes. Over the query cubes whose tiles lie in one block of 8 consecutive tiles, the distinct listed cubes whose tiles lie in any one block number 1 to 2; some block reaches 2 from every block. `queries`: of order one, up to 72 in magnitude. `keys_in`: of order one. `values`: of order one.
All inputs are finite; a program needn't handle non-finite values.
Results may differ from a plain program's by a relative error of at most 0.014.
Values may be sent and summed in bfloat16 or wider, within the bound.
A program may use at most 192 MiB of HBM per device.

v0:
```python
import math

import jax
import jax.numpy as jnp
from jax import lax
from jax.sharding import PartitionSpec as P


def lookup_table(table, indices):
    positions = jnp.arange(table.shape[0], dtype=jnp.int32)
    return jnp.sum(jnp.where(indices[..., None] == positions, table, 0), axis=-1)


def attend_back(query_rows, key_rows, value_rows, grad_rows, factor):
    scores = (
        jnp.einsum("tqd,tkd->tqk", query_rows, key_rows, preferred_element_type=jnp.float32)
        * factor
    )
    probs = jax.nn.softmax(scores, axis=-1)
    probs_low = probs.astype(jnp.bfloat16)
    dprobs = jnp.einsum("tqd,tkd->tqk", grad_rows, value_rows, preferred_element_type=jnp.float32)
    inner = jnp.sum(probs * dprobs, axis=-1, keepdims=True)
    dscores = (probs * (dprobs - inner)).astype(jnp.bfloat16)
    grad_query = (
        jnp.einsum("tqk,tkd->tqd", dscores, key_rows, preferred_element_type=jnp.float32) * factor
    )
    grad_key = (
        jnp.einsum("tqk,tqd->tkd", dscores, query_rows, preferred_element_type=jnp.float32) * factor
    )
    grad_value = jnp.einsum(
        "tqk,tqd->tkd", probs_low, grad_rows, preferred_element_type=jnp.float32
    )
    return (grad_query, grad_key, grad_value)


def coarse_back(query_rows, key_rows, value_rows, grad_rows, heads_dev, factor):

    def split_heads(rows):
        return rows.reshape(rows.shape[0], heads_dev, -1).transpose(1, 0, 2)

    def join_heads(rows):
        return rows.transpose(1, 0, 2).reshape(rows.shape[1], -1)

    grad_query, grad_key, grad_value = attend_back(
        split_heads(query_rows),
        split_heads(key_rows),
        split_heads(value_rows),
        split_heads(grad_rows),
        factor,
    )
    return (join_heads(grad_query), join_heads(grad_key), join_heads(grad_value))


def on_device(queries, keys_in, values, grad_out, fine_gate, coarse_gate, tile_of_cube, select):
    queries, keys_in, values, grad_out, fine_gate, coarse_gate = (
        lax.all_to_all(queries, "head", split_axis=1, concat_axis=0, tiled=True),
        lax.all_to_all(keys_in, "head", split_axis=1, concat_axis=0, tiled=True),
        lax.all_to_all(values, "head", split_axis=1, concat_axis=0, tiled=True),
        lax.all_to_all(grad_out, "head", split_axis=1, concat_axis=0, tiled=True),
        lax.all_to_all(fine_gate, "head", split_axis=1, concat_axis=0, tiled=True),
        lax.all_to_all(coarse_gate, "head", split_axis=1, concat_axis=0, tiled=True),
    )
    blocks = lax.axis_size("tok")
    member = lax.axis_index("tok")
    cubes = select.shape[0]
    topk = select.shape[1]
    cubes_dev = cubes // blocks
    tokens = queries.shape[0]
    cube = tokens // cubes_dev
    heads_dev = fine_gate.shape[1]
    width = queries.shape[1]
    hdim = width // heads_dev
    capacity = max(2, 2 * ((topk + blocks - 1) // blocks))
    factor = 1.0 / math.sqrt(hdim)
    grad_heads = grad_out.reshape(tokens, heads_dev, hdim)
    fine_grad = (
        (fine_gate[:, :, None] * grad_heads.astype(jnp.float32))
        .astype(jnp.bfloat16)
        .reshape(cubes_dev, cube, width)
    )
    coarse_terms = (coarse_gate[:, :, None] * grad_heads.astype(jnp.float32)).reshape(
        cubes_dev, cube, width
    )
    query_tiles = queries.reshape(cubes_dev, cube, width)
    key_tiles = keys_in.reshape(cubes_dev, cube, width)
    value_tiles = values.reshape(cubes_dev, cube, width)
    pooled_q = jnp.mean(query_tiles, axis=1, dtype=jnp.float32).astype(jnp.bfloat16)
    pooled_k = jnp.mean(key_tiles, axis=1, dtype=jnp.float32).astype(jnp.bfloat16)
    pooled_v = jnp.mean(value_tiles, axis=1, dtype=jnp.float32).astype(jnp.bfloat16)
    pooled_g = jnp.sum(coarse_terms, axis=1).astype(jnp.bfloat16)
    tiles = jnp.arange(cubes, dtype=jnp.int32)
    matches = tile_of_cube[None, :] == tiles[:, None]
    cube_of_tile = jnp.sum(jnp.where(matches, tiles[None, :], 0), axis=1)
    listed = jnp.take(select, cube_of_tile, axis=0)
    chosen = jnp.take(tile_of_cube, listed, axis=0)
    hits = jnp.any(chosen[:, :, None] == tiles[None, None, :], axis=1)
    needed = jnp.any(hits.reshape(blocks, cubes_dev, blocks, cubes_dev), axis=1)
    ranks = jnp.cumsum(needed.astype(jnp.int32), axis=2) - 1
    needed_here = lax.dynamic_index_in_dim(needed, member, axis=1, keepdims=False)
    ranks_here = lax.dynamic_index_in_dim(ranks, member, axis=1, keepdims=False)
    slot_numbers = jnp.arange(capacity, dtype=jnp.int32)
    packing = (
        (needed_here[:, None, :] & (ranks_here[:, None, :] == slot_numbers[None, :, None]))
        .reshape(blocks * capacity, cubes_dev)
        .astype(jnp.bfloat16)
    )
    own_chosen = lax.dynamic_slice_in_dim(chosen, member * cubes_dev, cubes_dev, 0)
    my_ranks = lax.dynamic_index_in_dim(ranks, member, axis=0, keepdims=False).reshape(cubes)
    slot_index = own_chosen // cubes_dev * capacity + lookup_table(my_ranks, own_chosen)
    packed_keys = (
        jnp.dot(
            packing, key_tiles.reshape(cubes_dev, cube * width), preferred_element_type=jnp.float32
        )
        .astype(jnp.bfloat16)
        .reshape(blocks, capacity, cube, width)
    )
    packed_values = (
        jnp.dot(
            packing,
            value_tiles.reshape(cubes_dev, cube * width),
            preferred_element_type=jnp.float32,
        )
        .astype(jnp.bfloat16)
        .reshape(blocks, capacity, cube, width)
    )
    fetched_keys, fetched_values = (
        lax.all_to_all(packed_keys, "tok", split_axis=0, concat_axis=0, tiled=True),
        lax.all_to_all(packed_values, "tok", split_axis=0, concat_axis=0, tiled=True),
    )
    source_keys = fetched_keys.reshape(blocks * capacity, cube, width)
    source_values = fetched_values.reshape(blocks * capacity, cube, width)
    flat_index = slot_index.reshape(-1)
    slot_flat = slot_index.reshape(-1)
    slot_count = blocks * capacity
    query_parts = []
    key_parts = []
    value_parts = []
    for head_num in range(heads_dev):
        start_col = head_num * hdim
        stop_col = start_col + hdim
        query_head = lax.slice_in_dim(query_tiles, start_col, stop_col, axis=2)
        grad_head = lax.slice_in_dim(fine_grad, start_col, stop_col, axis=2)
        keys_head = jnp.take(
            lax.slice_in_dim(source_keys, start_col, stop_col, axis=2), flat_index, axis=0
        ).reshape(cubes_dev, topk * cube, hdim)
        values_head = jnp.take(
            lax.slice_in_dim(source_values, start_col, stop_col, axis=2), flat_index, axis=0
        ).reshape(cubes_dev, topk * cube, hdim)
        grad_query, grad_key, grad_value = attend_back(
            query_head, keys_head, values_head, grad_head, factor
        )
        query_parts.append(grad_query)
        slot_key = jax.ops.segment_sum(
            grad_key.reshape(cubes_dev * topk, cube * hdim), slot_flat, num_segments=slot_count
        )
        slot_value = jax.ops.segment_sum(
            grad_value.reshape(cubes_dev * topk, cube * hdim), slot_flat, num_segments=slot_count
        )
        key_parts.append(slot_key.astype(jnp.bfloat16).reshape(slot_count, cube, hdim))
        value_parts.append(slot_value.astype(jnp.bfloat16).reshape(slot_count, cube, hdim))
    fine_dq = jnp.concatenate(query_parts, axis=2)
    slot_keys = jnp.concatenate(key_parts, axis=2).reshape(blocks, capacity, cube, width)
    slot_values = jnp.concatenate(value_parts, axis=2).reshape(blocks, capacity, cube, width)
    home_keys, home_values = (
        lax.all_to_all(slot_keys, "tok", split_axis=0, concat_axis=0, tiled=True),
        lax.all_to_all(slot_values, "tok", split_axis=0, concat_axis=0, tiled=True),
    )
    unpacking = packing.T
    fine_dk = jnp.dot(
        unpacking,
        home_keys.reshape(blocks * capacity, cube * width),
        preferred_element_type=jnp.float32,
    ).reshape(cubes_dev, cube, width)
    fine_dv = jnp.dot(
        unpacking,
        home_values.reshape(blocks * capacity, cube * width),
        preferred_element_type=jnp.float32,
    ).reshape(cubes_dev, cube, width)
    every_k, every_v = (
        lax.all_gather(pooled_k, "tok", axis=0, tiled=True),
        lax.all_gather(pooled_v, "tok", axis=0, tiled=True),
    )
    coarse_dq, partial_dk, partial_dv = coarse_back(
        pooled_q, every_k, every_v, pooled_g, heads_dev, factor
    )
    coarse_dk, coarse_dv = (
        lax.psum_scatter(
            partial_dk.astype(jnp.bfloat16), "tok", scatter_dimension=0, tiled=True
        ).astype(jnp.float32),
        lax.psum_scatter(
            partial_dv.astype(jnp.bfloat16), "tok", scatter_dimension=0, tiled=True
        ).astype(jnp.float32),
    )
    grad_queries = (
        (fine_dq + coarse_dq[:, None, :] / cube).astype(jnp.bfloat16).reshape(tokens, width)
    )
    grad_keys = (fine_dk + coarse_dk[:, None, :] / cube).astype(jnp.bfloat16).reshape(tokens, width)
    grad_values = (
        (fine_dv + coarse_dv[:, None, :] / cube).astype(jnp.bfloat16).reshape(tokens, width)
    )
    return (
        lax.all_to_all(grad_queries, "head", split_axis=0, concat_axis=1, tiled=True),
        lax.all_to_all(grad_keys, "head", split_axis=0, concat_axis=1, tiled=True),
        lax.all_to_all(grad_values, "head", split_axis=0, concat_axis=1, tiled=True),
    )


def solution(mesh):
    in_specs = (
        P(("tok", "head"), None),
        P(("tok", "head"), None),
        P(("tok", "head"), None),
        P(("tok", "head"), None),
        P(("tok", "head"), None),
        P(("tok", "head"), None),
        P(),
        P(),
    )
    out_specs = (P(("tok", "head"), None), P(("tok", "head"), None), P(("tok", "head"), None))
    return jax.shard_map(
        on_device, mesh=mesh, in_specs=in_specs, out_specs=out_specs, check_vma=False
    )
```

profile of v0, /device:TPU:1, one launch (start us, length us, event | category | flops | bytes accessed | tf_op | source)
XLA Modules:
  0.0 1086.2 jit_solution(4686357720591603388)
XLA Ops:
  8.7 5.9 all-to-all-start.7
  33.3 6.6 all-to-all-done
  43.7 25.7 %gather_fusion.1 = s32[4096]{0:T(1024)S(1)} fusion(s32[256]{0:T(256)S(1)} %copy-done, s32[4096]{0:T(1024)S(1)} %broadcast_clamp_fusion), kind=kCustom, calls=%fused_computation.11 | custom fusion | bytes 49152 | tf_op jit(solution)/shard_map/jit(_take)/gather | solution.py:95
  102.0 17.4 %all-to-all-start.1 = ((bf16[32,2,64,640]{3,2,1,0:T(8,128)(2,1)}), bf16[32,2,64,640]{3,2,1,0:T(8,128)(2,1)}, u32[]{:S(2)}, u32[]{:S(2)}) async-start(bf16[32,2,64,640]{3,2,1,0:T(8,128)(2,1)} %bitcast.338), calls=%async_computation.1 | async-start | bytes 10485760 | tf_op jit(solution)/shard_map/all_to_all | solution.py:127
  124.7 113.7 %all-to-all-done.1 = bf16[32,2,64,640]{3,2,1,0:T(8,128)(2,1)} async-done(((bf16[32,2,64,640]{3,2,1,0:T(8,128)(2,1)}), bf16[32,2,64,640]{3,2,1,0:T(8,128)(2,1)}, u32[]{:S(2)}, u32[]{:S(2)}) %all-to-all-start.1) | async-done | bytes 5242912 | tf_op jit(solution)/shard_map/all_to_all | solution.py:127
  238.5 5.4 all-to-all-start.6
  254.9 136.5 %all_gather.6 = bf16[256,640]{1,0:T(8,128)(2,1)S(1)} all-gather(bf16[8,640]{1,0:T(8,128)(2,1)S(1)} %multiply_convert_fusion.7), channel_id=1, replica_groups=mesh['head'=8,'tok'=32] {'tok'}, dimensions={0}, use_global_device_ids=true | all-gather | bytes 337920 | tf_op jit(solution)/shard_map/all_gather | solution.py:180
  391.9 40.0 %all_gather.7 = bf16[256,640]{1,0:T(8,128)(2,1)S(1)} all-gather(bf16[8,640]{1,0:T(8,128)(2,1)S(1)} %multiply_convert_fusion.6), channel_id=1, replica_groups=mesh['head'=8,'tok'=32] {'tok'}, dimensions={0}, use_global_device_ids=true | all-gather | bytes 337920 | tf_op jit(solution)/shard_map/all_gather | solution.py:181
  479.7 11.8 %broadcast_select_fusion.1 = (bf16[128,64,128]{2,1,0:T(8,128)(2,1)S(1)}, bf16[128,64,128]{2,1,0:T(8,128)(2,1)}, bf16[128,64,128]{2,1,0:T(8,128)(2,1)S(1)}, bf16[...) fusion(bf16[128,64,128]{2,1,0:T(8,128)(2,1)} %gather_fusion.10,, ...), kind=kLoop, calls=%fused_computation.74 | loop fusion | flops 10485760 | bytes 41943168 | tf_op jit(solution)/shard_map/jit(_take)/select_n | solution.py:143
  540.8 7.5 scatter_custom_fusion
  554.7 7.5 scatter_custom_fusion.1
  567.6 7.5 scatter_custom_fusion.2
  581.3 7.5 scatter_custom_fusion.3
  590.0 5.4 reshape.629
  595.3 7.5 scatter_custom_fusion.4
  611.7 8.9 all-to-all-start.9
  620.6 6.0 fusion.69
  631.6 7.5 scatter_custom_fusion.5
  639.6 6.0 fusion.67
  650.7 7.5 scatter_custom_fusion.6
  659.7 6.0 fusion.65
  671.0 7.5 scatter_custom_fusion.7
  679.9 6.0 fusion.63
  685.9 5.4 reshape.661
  691.3 7.5 scatter_custom_fusion.8
  700.3 6.1 fusion.61
  711.5 7.5 scatter_custom_fusion.9
  725.0 14.5 %all-to-all-done.9 = bf16[32,2,64,640]{3,2,1,0:T(8,128)(2,1)} async-done(((bf16[32,2,64,640]{3,2,1,0:T(8,128)(2,1)}), bf16[32,2,64,640]{3,2,1,0:T(8,128)(2,1)}, u32[]{:S(2)}, u32[]{:S(2)}) %all-to-all-start.9) | async-done | bytes 5242912 | tf_op jit(solution)/shard_map/all_to_all | solution.py:165
  748.0 290.6 %all-reduce.5.cloned.1.call-done = (bf16[256,640]{0,1:T(8,128)(2,1)}, bf16[256,640]{0,1:T(8,128)(2,1)}) async-done(((bf16[256,640]{0,1:T(8,128)(2,1)}, bf16[256,640]{0,1:T(8,128)(2,1)}), (bf16[256,640]{0,1:T(8,128)(2,1)}, bf16[256,640]{0,1:T(8,128)(2,1)})) %all-reduce.5.cloned.1.call-update) | async-done | bytes 655376
  1040.0 6.5 fusion.47
  1051.7 6.5 fusion.44
  1069.5 8.6 all-to-all-done.12
  (234 shorter events, 255.4 us)
Async XLA Ops:
  7.2 24.3 %copy-start = (s32[256]{0:T(256)S(1)}, s32[256]{0:T(256)}, u32[]{:S(2)}) copy-start(s32[256]{0:T(256)} %param.16) | copy-start | bytes 3076
  7.2 24.4 %copy-start.23 = (s32[256,16]{0,1:T(8,128)S(1)}, s32[256,16]{0,1:T(8,128)}, u32[]{:S(2)}) copy-start(s32[256,16]{0,1:T(8,128)} %param.17) | copy-start | bytes 49156
  7.2 24.5 %copy-start.18 = (bf16[64,5120]{1,0:T(8,128)(2,1)S(1)}, bf16[64,5120]{1,0:T(8,128)(2,1)}, u32[]{:S(2)}) copy-start(bf16[64,5120]{1,0:T(8,128)(2,1)} %param.12) | copy-start | bytes 1966084
  8.7 10.9 %all-to-all-start.7 = ((bf16[8,2,160]{2,1,0:T(2,128)(2,1)}), bf16[8,2,160]{2,1,0:T(2,128)(2,1)S(1)}, u32[]{:S(2)}, u32[]{:S(2)}) async-start(bf16[8,2,160]{2,1,0:T(2,128)(2,1)} %reshape.744), calls=%async_computation.7 | async-start | bytes 16384 | tf_op jit(solution)/shard_map/all_to_all | solution.py:61
  19.6 8.3 all-to-all-start.3
  27.9 12.0 %all-to-all-start = ((bf16[64,8,640]{2,0,1:T(8,128)(2,1)}), bf16[64,8,640]{2,0,1:T(8,128)(2,1)S(1)}, u32[]{:S(2)}, u32[]{:S(2)}) async-start(bf16[64,8,640]{2,0,1:T(8,128)(2,1)} %bitcast.335), calls=%async_computation | async-start | bytes 1310720 | tf_op jit(solution)/shard_map/all_to_all | solution.py:57
  39.9 30.7 %all-to-all-start.5 = ((bf16[64,8,640]{2,0,1:T(8,128)(2,1)}), bf16[64,8,640]{2,0,1:T(8,128)(2,1)S(1)}, u32[]{:S(2)}, u32[]{:S(2)}) async-start(bf16[64,8,640]{2,0,1:T(8,128)(2,1)} %bitcast.332), calls=%async_computation.5 | async-start | bytes 1310720 | tf_op jit(solution)/shard_map/all_to_all | solution.py:58
  43.7 25.9 %copy-start.19 = (bf16[64,5120]{1,0:T(8,128)(2,1)S(1)}, bf16[64,5120]{1,0:T(8,128)(2,1)}, u32[]{:S(2)}) copy-start(bf16[64,5120]{1,0:T(8,128)(2,1)} %param.10) | copy-start | bytes 1966084
  70.6 17.3 %all-to-all-start.2 = ((bf16[64,8,640]{2,0,1:T(8,128)(2,1)}), bf16[64,8,640]{2,0,1:T(8,128)(2,1)S(1)}, u32[]{:S(2)}, u32[]{:S(2)}) async-start(bf16[64,8,640]{2,0,1:T(8,128)(2,1)} %bitcast.334), calls=%async_computation.2 | async-start | bytes 1310720 | tf_op jit(solution)/shard_map/all_to_all | solution.py:56
  88.6 13.4 %all-to-all-start.4 = ((bf16[64,8,640]{2,0,1:T(8,128)(2,1)}), bf16[64,8,640]{2,0,1:T(8,128)(2,1)S(1)}, u32[]{:S(2)}, u32[]{:S(2)}) async-start(bf16[64,8,640]{2,0,1:T(8,128)(2,1)} %bitcast.374), calls=%async_computation.4 | async-start | bytes 1310720 | tf_op jit(solution)/shard_map/all_to_all | solution.py:59
  93.8 25.9 %copy-start.21 = (pred[64,8]{1,0:T(32,128)(4,1)}, pred[64,8]{1,0:T(32,128)(4,1)S(1)}, u32[]{:S(2)}) copy-start(pred[64,8]{1,0:T(32,128)(4,1)S(1)} %and.65) | copy-start | bytes 1540
  102.0 136.5 %all-to-all-start.1 = ((bf16[32,2,64,640]{3,2,1,0:T(8,128)(2,1)}), bf16[32,2,64,640]{3,2,1,0:T(8,128)(2,1)}, u32[]{:S(2)}, u32[]{:S(2)}) async-start(bf16[32,2,64,640]{3,2,1,0:T(8,128)(2,1)} %bitcast.338), calls=%async_computation.1 | async-start | bytes 10485760 | tf_op jit(solution)/shard_map/all_to_all | solution.py:127
  238.5 203.6 %all-to-all-start.6 = ((bf16[32,2,64,640]{3,2,1,0:T(8,128)(2,1)}), bf16[32,2,64,640]{3,2,1,0:T(8,128)(2,1)}, u32[]{:S(2)}, u32[]{:S(2)}) async-start(bf16[32,2,64,640]{3,2,1,0:T(8,128)(2,1)} %bitcast.337), calls=%async_computation.6 | async-start | bytes 10485760 | tf_op jit(solution)/shard_map/all_to_all | solution.py:128
  492.4 1.7 copy-start.1
  492.4 2.3 copy-start.16
  492.4 2.5 copy-start.17
  500.3 2.1 copy-start.2
  500.3 2.3 copy-start.15
  508.1 2.4 copy-start.14
  515.9 2.3 copy-start.13
  523.7 1.7 copy-start.5
  523.7 2.3 copy-start.12
  531.5 80.2 %all-to-all-start.8 = ((bf16[8,64,640]{2,1,0:T(8,128)(2,1)}), bf16[8,64,640]{2,1,0:T(8,128)(2,1)}, u32[]{:S(2)}, u32[]{:S(2)}) async-start(bf16[8,64,640]{2,1,0:T(8,128)(2,1)} %add_convert_fusion), calls=%async_computation.8 | async-start | bytes 1310720 | tf_op jit(solution)/shard_map/all_to_all | solution.py:202
  611.7 127.8 %all-to-all-start.9 = ((bf16[32,2,64,640]{3,2,1,0:T(8,128)(2,1)}), bf16[32,2,64,640]{3,2,1,0:T(8,128)(2,1)}, u32[]{:S(2)}, u32[]{:S(2)}) async-start(bf16[32,2,64,640]{3,2,1,0:T(8,128)(2,1)} %constant_dynamic-update-slice_fusion), calls=%async_computation.9 | async-start | bytes 10485760 | tf_op jit(solution)/shard_map/all_to_all | solution.py:165
  719.5 2.2 copy-start.9
  720.7 2.2 copy-start.11
  725.0 21.7 %copy-start.24 = (u32[256]{0:T(256)S(1)}, u32[256]{0:T(256)}, u32[]{:S(2)}) copy-start(u32[256]{0:T(256)} %constant.115) | copy-start | bytes 3076
  739.5 307.9 %all-to-all-start.11 = ((bf16[32,2,64,640]{3,2,1,0:T(8,128)(2,1)}), bf16[32,2,64,640]{3,2,1,0:T(8,128)(2,1)}, u32[]{:S(2)}, u32[]{:S(2)}) async-start(bf16[32,2,64,640]{3,2,1,0:T(8,128)(2,1)} %constant_dynamic-update-slice_fusion.5), calls=%async_computation.11 | async-start | bytes 10485760 | tf_op jit(solution)/shard_map/all_to_all | solution.py:166
  744.6 295.4 %copy-start.22 = (pred[64,8]{1,0:T(32,128)(4,1)S(1)}, pred[64,8]{1,0:T(32,128)(4,1)}, u32[]{:S(2)}) copy-start(pred[64,8]{1,0:T(32,128)(4,1)} %copy-done.21) | copy-start | bytes 1540
  744.6 294.0 %all-reduce.5.cloned.1.call-start = ((), (), s32[]{:S(2)}) async-start(), calls=%async_computation.13 | async-start | bytes 1310720
  1047.4 15.7 %all-to-all-start.10 = ((bf16[8,64,640]{2,1,0:T(8,128)(2,1)}), bf16[8,64,640]{2,1,0:T(8,128)(2,1)S(1)}, u32[]{:S(2)}, u32[]{:S(2)}) async-start(bf16[8,64,640]{2,1,0:T(8,128)(2,1)} %copy.147), calls=%async_computation.10 | async-start | bytes 1310720 | tf_op jit(solution)/shard_map/all_to_all | solution.py:203
  1063.1 15.1 %all-to-all-start.12 = ((bf16[8,64,640]{2,1,0:T(8,128)(2,1)}), bf16[8,64,640]{2,1,0:T(8,128)(2,1)S(1)}, u32[]{:S(2)}, u32[]{:S(2)}) async-start(bf16[8,64,640]{2,1,0:T(8,128)(2,1)} %copy.152), calls=%async_computation.12 | async-start | bytes 1310720 | tf_op jit(solution)/shard_map/all_to_all | solution.py:204
  (7 other events, 9.7 us)
Sparse Core Ops, SparseCore 0:
  748.7 289.8 all-reduce.4
where the time goes:
time: 1100 us; the launch traced here: 1090 us
  waiting for transfers between devices  448 us (41%)
  local copies, waits for them, and re-layouts  182 us (17%)
  blocking collectives  177 us (16%)
  other arithmetic  115 us (10%)
  starting transfers between devices  75.4 us (7%)
  matrix products  73.8 us (7%)
  between operations  15.9 us (1%)
    unnamed x2, waiting for transfers between devices  291 us
    all_gather x1, blocking collectives, on_device(): lax.all_gather(pooled_k, 'tok', axis=0, tiled=True)  136 us
    all_to_all x1, waiting for transfers between devices, on_device(): lax.all_to_all(packed_keys, 'tok', split_axis=0, concat_axis=0, tiled=True)  114 us
    all_gather x1, blocking collectives, on_device(): lax.all_gather(pooled_v, 'tok', axis=0, tiled=True)  40 us
    scatter-add x5, other arithmetic, on_device(): jax.ops.segment_sum(grad_key.reshape(cubes_dev * topk, cube * hdim), slot...  37.7 us
    scatter-add x5, other arithmetic, on_device(): jax.ops.segment_sum(grad_value.reshape(cubes_dev * topk, cube * hdim), sl...  37.7 us
    unnamed x79, local copies, waits for them, and re-layouts  32.2 us
    dot_general x6, matrix products, attend_back(): jnp.einsum('tqk,tqd->tkd', probs_low, grad_rows, preferred_element_type=j...  31.1 us
  transfers between devices with their start and end apart: 14, of which 9 were waited for; matrix products, arithmetic and copies ran while one was open for 25% of the time, Pallas kernels for 0%

commit v1 on v0

v1 whole, which is shorter than its diff:
```python
import functools
import math

import jax
import jax.numpy as jnp
from jax import lax
from jax.experimental import pallas as pl
from jax.experimental.pallas import tpu as pltpu
from jax.sharding import PartitionSpec as P

MESH = pl.DeviceIdType.MESH
BF16 = jnp.bfloat16
F32 = jnp.float32

CUBE = 64
HDIM = 128
PLANES = 8
CHIPS = 16
HEADS_PLANE = 5
COPIES = 3
WORKERS = HEADS_PLANE * COPIES
WIDTH = HEADS_PLANE * HDIM
QGROUPS = 6
TOPK = 16
SLOTS = 2 * CHIPS * PLANES
UNITS = QGROUPS * PLANES
HALF = CUBE // 2
STAGES = 8
ATTEND_VMEM = 30 * 2**20
HOME_VMEM = 20 * 2**20


def where_am_i():
    tok = lax.axis_index("tok")
    head = lax.axis_index("head")
    plane = tok // 4
    chip = (tok // 2) % 2 * 8 + head
    core = tok % 2
    return plane, chip, core


def head_of(chip):
    return jnp.minimum(chip // COPIES, HEADS_PLANE - 1)


def device_of(plane, chip, core):
    return {"tok": plane * 4 + chip // 8 * 2 + core, "head": chip % 8}


def remote(src, dst, send, recv, device):
    return pltpu.make_async_remote_copy(
        src_ref=src, dst_ref=dst, send_sem=send, recv_sem=recv, device_id=device, device_id_type=MESH
    )


def take_bytes(ref, sem):
    pltpu.make_async_copy(ref, ref, sem).wait()


def greet(plane, chip, core):
    barrier = pltpu.get_barrier_semaphore()

    def along_z(d, _):
        pl.semaphore_signal(
            barrier, inc=1, device_id=device_of((plane + d) % PLANES, chip, core), device_id_type=MESH
        )
        return 0

    def in_plane(d, _):
        pl.semaphore_signal(
            barrier, inc=1, device_id=device_of(plane, (chip + d) % CHIPS, core), device_id_type=MESH
        )
        return 0

    lax.fori_loop(1, PLANES, along_z, 0)
    lax.fori_loop(1, CHIPS, in_plane, 0)
    pl.semaphore_signal(
        barrier, inc=1, device_id=device_of(plane, chip, 1 - core), device_id_type=MESH
    )
    pl.semaphore_wait(barrier, PLANES - 1 + CHIPS - 1 + 1)


def columns(group, width=WIDTH):
    return pl.ds(pl.multiple_of(group * width, 128), width)


def rows_of(half):
    return pl.ds(half * HALF, HALF)


def bring_kernel(
    k_in, v_in, q_in, g_hbm, fgate, cgate,
    kh, vh, qh, fh, ph,
    kz, vz, qz, fz, pz, fg, pg, g_in,
    gsem, zsend, zrecv, psend, krecv, qrecv, fsend, frecv,
):
    plane, chip, core = where_am_i()
    load_grad = pltpu.make_async_copy(g_hbm, g_in, gsem)
    load_grad.start()
    greet(plane, chip, core)

    def start_along_z(stage, source, landing):
        def step(d, _):
            target = (plane + d) % PLANES
            remote(
                source(target), landing(plane), zsend.at[stage], zrecv.at[stage],
                device_of(target, chip, core),
            ).start()
            return 0

        lax.fori_loop(1, PLANES, step, 0)
        pltpu.make_async_copy(source(plane), landing(plane), zrecv.at[stage]).start()

    sources = (
        lambda t, rows: k_in.at[rows, columns(t)],
        lambda t, rows: v_in.at[rows, columns(t)],
        lambda t, rows: q_in.at[rows, columns(t)],
        lambda t, rows: fg.at[t, rows],
    )
    slabs = (kz, vz, qz, fz)
    outs = (kh, vh, qh, fh)

    def start_stage(stage):
        number, rows = stage // 2, rows_of(stage % 2)
        start_along_z(
            stage, lambda t: sources[number](t, rows), lambda t: slabs[number].at[t, rows]
        )

    start_stage(0)
    start_stage(1)
    load_grad.wait()

    def gates(group, _):
        row = lax.broadcasted_iota(jnp.int32, (fgate.shape[0], WIDTH), 0)
        col = lax.broadcasted_iota(jnp.int32, (fgate.shape[0], WIDTH), 1)
        spread = jnp.where(
            row == group * HEADS_PLANE + lax.shift_right_logical(col, 7), 1.0, 0.0
        ).astype(BF16)
        grad = g_in[:, columns(group)].astype(F32)
        fine = tn(fgate[...], spread)
        fg[group] = (fine * grad).astype(BF16)
        coarse = tn(cgate[...], spread)
        pooled = jnp.sum(coarse * grad, axis=0, keepdims=True)
        rows = [pooled[:, j * HDIM:(j + 1) * HDIM] for j in range(HEADS_PLANE)]
        rows.append(jnp.zeros((16 - HEADS_PLANE, HDIM), F32))
        pg[group] = jnp.concatenate(rows, axis=0).astype(BF16)
        return 0

    lax.fori_loop(0, PLANES, gates, 0)

    def share_keys(number, rows):
        landed, out = slabs[number], outs[number]

        def step(d, _):
            target = (chip + d) % CHIPS

            @pl.when(target < WORKERS)
            def _():
                remote(
                    landed.at[:, rows, columns(head_of(target), HDIM)],
                    out.at[core * CHIPS + chip, :, rows],
                    psend.at[number], krecv.at[number, chip], device_of(plane, target, core),
                ).start()

            return 0

        lax.fori_loop(1, CHIPS, step, 0)

        @pl.when(chip < WORKERS)
        def _():
            pltpu.make_async_copy(
                landed.at[:, rows, columns(head_of(chip), HDIM)],
                out.at[core * CHIPS + chip, :, rows],
                krecv.at[number, chip],
            ).start()

    def share_queries(number, pick, place):
        def step(j, _):
            target = j * COPIES + chip % COPIES

            @pl.when(target != chip)
            def _():
                remote(
                    pick(j), place(chip // COPIES), psend.at[number],
                    qrecv.at[number - 2], device_of(plane, target, core),
                ).start()

            @pl.when(target == chip)
            def _():
                pltpu.make_async_copy(
                    pick(j), place(chip // COPIES), qrecv.at[number - 2]
                ).start()

            return 0

        lax.fori_loop(0, HEADS_PLANE, step, 0)

    for stage in range(STAGES):
        number, rows = stage // 2, rows_of(stage % 2)
        take_bytes(slabs[number].at[:, rows], zrecv.at[stage])
        if stage + 2 < STAGES:
            start_stage(stage + 2)
        if stage + 2 == STAGES:
            start_along_z(STAGES, lambda t: pg.at[t], lambda t: pz.at[t])
        if number < 2:
            share_keys(number, rows)
        else:
            share_queries(
                number,
                lambda j, number=number, rows=rows: slabs[number].at[:, rows, columns(j, HDIM)],
                lambda i, number=number, rows=rows: outs[number].at[i, :, rows],
            )
    take_bytes(pz, zrecv.at[STAGES])
    share_queries(4, lambda j: pz, lambda i: ph.at[i])

    sibling = device_of(plane, chip, 1 - core)

    @pl.when(chip < WORKERS)
    def _():
        for number, out in ((0, kh), (1, vh)):
            def forward(d, _, number=number, out=out):
                origin = (chip + CHIPS - d) % CHIPS
                block = out.at[core * CHIPS + origin]
                take_bytes(block, krecv.at[number, origin])
                remote(block, block, fsend.at[number], frecv.at[number], sibling).start()
                return 0

            lax.fori_loop(0, CHIPS, forward, 0)

        @pl.when(chip % COPIES == 0)
        def _():
            for number, out in enumerate((qh, fh, ph)):
                take_bytes(out, qrecv.at[number])

        @pl.when(chip % COPIES != 0)
        def _():
            for number, out in enumerate((qh, fh, ph)):
                take_bytes(out.at[pl.ds(0, QGROUPS - 1)], qrecv.at[number])

        for number, out in ((0, kh), (1, vh)):
            theirs = out.at[pl.ds((1 - core) * CHIPS, CHIPS)]
            take_bytes(theirs, frecv.at[number])
            take_bytes(theirs, fsend.at[number])

    for stage in range(STAGES):
        landed = slabs[stage // 2].at[pl.ds(0, PLANES - 1), rows_of(stage % 2)]
        take_bytes(landed, zsend.at[stage])
    take_bytes(pz.at[pl.ds(0, PLANES - 1)], zsend.at[STAGES])

    @pl.when(chip < WORKERS)
    def _():
        for number, out in ((0, kh), (1, vh)):
            take_bytes(out.at[pl.ds(0, WORKERS - 1)], psend.at[number])
        for number, out in ((2, qh), (3, fh), (4, ph)):
            take_bytes(out.at[pl.ds(0, HEADS_PLANE - 1)], psend.at[number])

    @pl.when(chip >= WORKERS)
    def _():
        for number, out in ((0, kh), (1, vh)):
            take_bytes(out.at[pl.ds(0, WORKERS)], psend.at[number])
        for number, out in ((2, qh), (3, fh), (4, ph)):
            take_bytes(out.at[pl.ds(0, HEADS_PLANE)], psend.at[number])


def bring(keys_in, values, queries, grad_out, fine_gate, coarse_gate):
    keys_shape = jax.ShapeDtypeStruct((2 * CHIPS, PLANES, CUBE, HDIM), BF16)
    query_shape = jax.ShapeDtypeStruct((QGROUPS, PLANES, CUBE, HDIM), BF16)
    pooled_shape = jax.ShapeDtypeStruct((QGROUPS, PLANES, 16, HDIM), BF16)
    anywhere = pl.BlockSpec(memory_space=pl.ANY)
    in_hbm = pl.BlockSpec(memory_space=pltpu.HBM)
    in_vmem = pl.BlockSpec(memory_space=pltpu.VMEM)
    slab = pltpu.VMEM((PLANES, CUBE, WIDTH), BF16)
    small = pltpu.VMEM((PLANES, 16, HDIM), BF16)
    return pl.pallas_call(
        bring_kernel,
        name="bring",
        out_shape=(keys_shape, keys_shape, query_shape, query_shape, pooled_shape),
        in_specs=[in_hbm] * 4 + [in_vmem] * 2,
        out_specs=[anywhere] * 5,
        scratch_shapes=[
            slab, slab, slab, slab, small, slab, small,
            pltpu.VMEM(grad_out.shape, BF16),
            pltpu.SemaphoreType.DMA,
            pltpu.SemaphoreType.DMA((STAGES + 1,)),
            pltpu.SemaphoreType.DMA((STAGES + 1,)),
            pltpu.SemaphoreType.DMA((5,)),
            pltpu.SemaphoreType.DMA((2, CHIPS)),
            pltpu.SemaphoreType.DMA((3,)),
            pltpu.SemaphoreType.DMA((2,)),
            pltpu.SemaphoreType.DMA((2,)),
        ],
        compiler_params=pltpu.CompilerParams(
            collective_id=0, has_side_effects=True, vmem_limit_bytes=16 * 2**20
        ),
    )(keys_in, values, queries, grad_out, fine_gate.T, coarse_gate.T)


def nt(a, b):
    return lax.dot_general(a, b, (((1,), (1,)), ((), ())), preferred_element_type=F32)


def tn(a, b):
    return lax.dot_general(a, b, (((0,), (0,)), ((), ())), preferred_element_type=F32)


def nn(a, b):
    return jnp.dot(a, b, preferred_element_type=F32)


def attend_kernel(
    toc, sel, q, fg, pg, k, v,
    dq, dk, dv,
    ak, av, pk, pv, pq, cdq, part, cot, soc,
):
    _, chip, core = where_am_i()
    head, replica = chip // COPIES, chip % COPIES
    groups = jnp.where(replica == 0, QGROUPS, QGROUPS - 1)
    groups = jnp.where(chip < WORKERS, groups, 0)
    units = groups * PLANES
    factor = 1.0 / math.sqrt(HDIM)
    log2e = math.log2(math.e)

    def invert(cube, _):
        tile = toc[cube]
        cot[tile] = cube
        soc[cube] = (
            lax.shift_left(lax.shift_right_logical(tile, 3) & 1, 7)
            + lax.shift_left(lax.shift_right_logical(tile, 4) & 1, 6)
            + lax.shift_left(tile & 7, 3)
            + lax.shift_right_logical(tile, 5)
        )
        return 0

    lax.fori_loop(0, SLOTS, invert, 0, unroll=8)

    def pool(source, groups, into):
        def gather(group, _):
            block = source[pl.ds(pl.multiple_of(group * 8, 8), 8)].astype(F32)
            halves = jnp.sum(block.reshape(8, 8, 8, HDIM), axis=1)
            part[pl.ds(pl.multiple_of(group * 64, 64), 64), :] = halves.reshape(64, HDIM)
            return 0

        lax.fori_loop(0, groups, gather, 0, unroll=2)
        count = into.shape[0]
        total = part[pl.ds(0, count, stride=8), :]
        for row in range(1, 8):
            total += part[pl.ds(row, count, stride=8), :]
        into[...] = total * (1.0 / CUBE)

    pool(k, SLOTS // 8, pk)
    pool(v, SLOTS // 8, pv)
    pool(q, UNITS // 8, pq)
    unit_at = lax.broadcasted_iota(jnp.int32, (UNITS, 16, HDIM), 0)
    row_at = lax.broadcasted_iota(jnp.int32, (UNITS, 16, HDIM), 1)
    pooled_g = jnp.sum(
        jnp.where((unit_at < units) & (row_at == head), pg[...].astype(F32), 0.0), axis=1
    ).astype(BF16)
    live = lax.broadcasted_iota(jnp.int32, (UNITS, HDIM), 0) < units
    pooled_q = jnp.where(live, pq[...], 0.0).astype(BF16)
    pooled_k = pk[...].astype(BF16)
    pooled_v = pv[...].astype(BF16)
    scores = nt(pooled_q, pooled_k) * factor
    weights = jnp.exp(scores - jnp.max(scores, axis=1, keepdims=True))
    probs = weights / jnp.sum(weights, axis=1, keepdims=True)
    dprobs = nt(pooled_g, pooled_v)
    inner = jnp.sum(probs * dprobs, axis=1, keepdims=True)
    dscores = (probs * (dprobs - inner)).astype(BF16)
    cdq[...] = nn(dscores, pooled_k) * (factor / CUBE)
    pk[...] = tn(dscores, pooled_q) * (1.0 / CUBE)
    pv[...] = tn(probs.astype(BF16), pooled_g) * (1.0 / CUBE)

    def fill(slot, _):
        ak[slot] = jnp.broadcast_to(pk[pl.ds(slot, 1), :], (CUBE, HDIM))
        av[slot] = jnp.broadcast_to(pv[pl.ds(slot, 1), :], (CUBE, HDIM))
        return 0

    lax.fori_loop(0, SLOTS, fill, 0, unroll=4)

    def listed(n):
        origin = n // PLANES * COPIES + replica
        tile = ((n % PLANES * 4) + origin // 8 * 2 + core) * 8 + origin % 8
        cube = cot[tile]
        slots = [soc[sel[r, cube]] for r in range(TOPK)]
        return [slots[c * 4:c * 4 + 4] for c in range(4)]

    def tiles_of(ref, quarter):
        return jnp.concatenate([ref[s] for s in quarter], axis=0)

    def softmax_terms(n, quarters):
        score = [nt(q[n], tiles_of(k, quarter)) for quarter in quarters]
        dprob = [nt(fg[n], tiles_of(v, quarter)) for quarter in quarters]
        top = functools.reduce(jnp.maximum, score)
        top = jnp.max(top, axis=1, keepdims=True)
        weight = [jnp.exp2((s - top) * (factor * log2e)) for s in score]
        total = jnp.sum(functools.reduce(jnp.add, weight), axis=1, keepdims=True)
        inverse = 1.0 / total
        mixed = functools.reduce(jnp.add, [w * d for w, d in zip(weight, dprob)])
        center = jnp.sum(mixed, axis=1, keepdims=True) * inverse
        probs = [w * inverse for w in weight]
        dscore = [(p * (d - center)).astype(BF16) for p, d in zip(probs, dprob)]
        return [p.astype(BF16) for p in probs], dscore

    def spread_terms(n, quarters, probs, dscore):
        query, grad = q[n], fg[n]
        dquery = jnp.zeros((CUBE, HDIM), F32)
        for c, quarter in enumerate(quarters):
            dquery += nn(dscore[c], tiles_of(k, quarter))
            key_terms = tn(dscore[c], query)
            value_terms = tn(probs[c], grad)
            for i, s in enumerate(quarter):
                ak[s] += key_terms[i * CUBE:(i + 1) * CUBE]
                av[s] += value_terms[i * CUBE:(i + 1) * CUBE]
        dq[n] = (dquery * factor + cdq[pl.ds(n, 1), :]).astype(BF16)

    def pair(m, _):
        numbers = [2 * m, 2 * m + 1]
        lists = [listed(n) for n in numbers]
        terms = [softmax_terms(n, quarters) for n, quarters in zip(numbers, lists)]
        for n, quarters, (probs, dscore) in zip(numbers, lists, terms):
            spread_terms(n, quarters, probs, dscore)
        return 0

    lax.fori_loop(0, units // 2, pair, 0)

    def finish(group, _):
        rows = pl.ds(pl.multiple_of(group * 4, 4), 4)
        dk[rows] = (ak[rows] * factor).astype(BF16)
        dv[rows] = av[rows].astype(BF16)
        return 0

    lax.fori_loop(0, SLOTS // 4, finish, 0)


def attend(tile_of_cube, select, qh, fh, ph, kh, vh):
    smem = pl.BlockSpec(memory_space=pltpu.SMEM)
    vmem = pl.BlockSpec(memory_space=pltpu.VMEM)
    query_shape = jax.ShapeDtypeStruct((UNITS, CUBE, HDIM), BF16)
    keys_shape = jax.ShapeDtypeStruct((SLOTS, CUBE, HDIM), BF16)
    return pl.pallas_call(
        attend_kernel,
        name="attend",
        out_shape=(query_shape, keys_shape, keys_shape),
        in_specs=[smem] * 2 + [vmem] * 5,
        out_specs=[vmem] * 3,
        scratch_shapes=[
            pltpu.VMEM((SLOTS, CUBE, HDIM), F32),
            pltpu.VMEM((SLOTS, CUBE, HDIM), F32),
            pltpu.VMEM((SLOTS, HDIM), F32),
            pltpu.VMEM((SLOTS, HDIM), F32),
            pltpu.VMEM((UNITS, HDIM), F32),
            pltpu.VMEM((UNITS, HDIM), F32),
            pltpu.VMEM((SLOTS * 8, HDIM), F32),
            pltpu.SMEM((SLOTS,), jnp.int32),
            pltpu.SMEM((SLOTS,), jnp.int32),
        ],
        compiler_params=pltpu.CompilerParams(vmem_limit_bytes=ATTEND_VMEM),
    )(
        tile_of_cube, select.T,
        qh.reshape(UNITS, CUBE, HDIM), fh.reshape(UNITS, CUBE, HDIM),
        ph.reshape(UNITS, 16, HDIM), kh.reshape(SLOTS, CUBE, HDIM), vh.reshape(SLOTS, CUBE, HDIM),
    )


def home_kernel(
    dq, dk, dv,
    oq, ok, ov,
    own_k, own_v, sib_k, sib_v, land_q, land_k, land_v, sum_k, sum_v,
    ssend, srecv, psend, precv, zsend, zrecv,
):
    plane, chip, core = where_am_i()
    head, replica = head_of(chip), chip % COPIES
    works = chip < WORKERS
    greet(plane, chip, core)
    sibling = device_of(plane, chip, 1 - core)
    sources, owns, sibs = (dk, dv), (own_k, own_v), (sib_k, sib_v)
    lands, sums, outs = (land_k, land_v), (sum_k, sum_v), (ok, ov)
    spread = columns(head, HDIM)
    mine = columns(plane)

    @pl.when(works)
    def _():
        for number in range(2):
            def give(d, _, number=number):
                target = (chip + d) % CHIPS
                remote(
                    sources[number].at[(1 - core) * CHIPS + target], sibs[number].at[target],
                    ssend.at[number], srecv.at[number, target], sibling,
                ).start()
                return 0

            lax.fori_loop(0, CHIPS, give, 0)

        def send_query(i, _):
            wanted = i * COPIES + replica
            target = jnp.minimum(wanted, CHIPS - 1)

            @pl.when((wanted < CHIPS) & (target != chip))
            def _():
                remote(
                    dq.at[i], land_q.at[:, :, spread], psend.at[2], precv.at[4],
                    device_of(plane, target, core),
                ).start()

            @pl.when(wanted == chip)
            def _():
                pltpu.make_async_copy(dq.at[i], land_q.at[:, :, spread], precv.at[4]).start()

            return 0

        lax.fori_loop(0, QGROUPS, send_query, 0)

    def settle(number, half):
        rows = rows_of(half)
        source, own, sib, land = sources[number], owns[number], sibs[number], lands[number]

        def step(d, _):
            target = (chip + d) % CHIPS
            if half == 0:
                take_bytes(sib.at[target], srecv.at[number, target])
            own[target, :, rows] = (
                source[core * CHIPS + target, :, rows].astype(F32)
                + sib[target, :, rows].astype(F32)
            ).astype(BF16)
            arrived = precv.at[number * 2 + half]

            @pl.when(target != chip)
            def _():
                remote(
                    own.at[target, :, rows], land.at[replica, :, rows, spread], psend.at[number],
                    arrived, device_of(plane, target, core),
                ).start()

            @pl.when(target == chip)
            def _():
                pltpu.make_async_copy(
                    own.at[target, :, rows], land.at[replica, :, rows, spread], arrived
                ).start()

            return 0

        @pl.when(works)
        def _():
            lax.fori_loop(0, CHIPS, step, 0)

    def send_home(number, block, out, target):
        @pl.when(target != plane)
        def _():
            remote(
                block, out, zsend.at[number], zrecv.at[number], device_of(target, chip, core)
            ).start()

        @pl.when(target == plane)
        def _():
            pltpu.make_async_copy(block, out, zrecv.at[number]).start()

    def queries_home():
        take_bytes(land_q, precv.at[4])

        def step(d, _):
            target = (plane + d) % PLANES
            send_home(2, land_q.at[target], oq.at[:, mine], target)
            return 0

        lax.fori_loop(0, PLANES, step, 0)

    def keys_home(number, half):
        rows = rows_of(half)
        land, total, out = lands[number], sums[number], outs[number]
        take_bytes(land.at[:, :, rows], precv.at[number * 2 + half])

        def step(d, _):
            target = (plane + d) % PLANES
            summed = land[0, target, rows].astype(F32)
            for r in range(1, COPIES):
                summed += land[r, target, rows].astype(F32)
            total[target, rows] = summed.astype(BF16)
            send_home(number, total.at[target, rows], out.at[rows, mine], target)
            return 0

        lax.fori_loop(0, PLANES, step, 0)

    settle(0, 0)
    settle(0, 1)
    queries_home()
    keys_home(0, 0)
    settle(1, 0)
    keys_home(0, 1)
    settle(1, 1)
    keys_home(1, 0)
    keys_home(1, 1)

    for number, out in enumerate((ok, ov, oq)):
        take_bytes(out, zrecv.at[number])
        take_bytes(land_q.at[pl.ds(0, PLANES - 1)], zsend.at[number])

    @pl.when(works)
    def _():
        for number in range(2):
            take_bytes(sibs[number], ssend.at[number])
            take_bytes(owns[number].at[pl.ds(0, CHIPS - 1)], psend.at[number])

        @pl.when(replica == 0)
        def _():
            take_bytes(dq.at[pl.ds(0, QGROUPS - 1)], psend.at[2])

        @pl.when(replica != 0)
        def _():
            take_bytes(dq.at[pl.ds(0, QGROUPS - 2)], psend.at[2])


def home(dq, dk, dv, rows, width):
    anywhere = pl.BlockSpec(memory_space=pl.ANY)
    in_vmem = pl.BlockSpec(memory_space=pltpu.VMEM)
    out_shape = jax.ShapeDtypeStruct((rows, width), BF16)
    half = pltpu.VMEM((CHIPS, PLANES, CUBE, HDIM), BF16)
    slab = pltpu.VMEM((PLANES, CUBE, WIDTH), BF16)
    slabs = pltpu.VMEM((COPIES, PLANES, CUBE, WIDTH), BF16)
    return pl.pallas_call(
        home_kernel,
        name="home",
        out_shape=(out_shape,) * 3,
        in_specs=[anywhere, in_vmem, in_vmem],
        out_specs=[anywhere] * 3,
        scratch_shapes=[
            half, half, half, half, slab, slabs, slabs, slab, slab,
            pltpu.SemaphoreType.DMA((2,)),
            pltpu.SemaphoreType.DMA((2, CHIPS)),
            pltpu.SemaphoreType.DMA((3,)),
            pltpu.SemaphoreType.DMA((5,)),
            pltpu.SemaphoreType.DMA((3,)),
            pltpu.SemaphoreType.DMA((3,)),
        ],
        compiler_params=pltpu.CompilerParams(
            collective_id=1, has_side_effects=True, vmem_limit_bytes=HOME_VMEM
        ),
    )(
        dq.reshape(QGROUPS, PLANES, CUBE, HDIM),
        dk.reshape(2 * CHIPS, PLANES, CUBE, HDIM),
        dv.reshape(2 * CHIPS, PLANES, CUBE, HDIM),
    )


def on_device(queries, keys_in, values, grad_out, fine_gate, coarse_gate, tile_of_cube, select):
    kh, vh, qh, fh, ph = bring(keys_in, values, queries, grad_out, fine_gate, coarse_gate)
    dq, dk, dv = attend(tile_of_cube, select, qh, fh, ph, kh, vh)
    return home(dq, dk, dv, *queries.shape)


def solution(mesh):
    split = P(("tok", "head"), None)
    return jax.shard_map(
        on_device,
        mesh=mesh,
        in_specs=(split,) * 6 + (P(), P()),
        out_specs=(split,) * 3,
        check_vma=False,
    )
```

time: 1100 us -> 208 us (0.19); the launches traced: 1090 us -> 207 us
  waiting for transfers between devices: 448 us -> 0 us
  Pallas kernels: 0 us -> 197 us
  blocking collectives: 177 us -> 0 us
  local copies, waits for them, and re-layouts: 182 us -> 9.65 us
  other arithmetic: 115 us -> 0 us
  starting transfers between devices: 75.4 us -> 0 us
  matrix products: 73.8 us -> 0 us
  between operations: 15.9 us -> 0.68 us
    unnamed x2 -> x0, waiting for transfers between devices: 291 us -> none
    pallas_call x0 -> x3, Pallas kernels: none -> 197 us  [the longest x1 85.9 us: bring(): pl.pallas_call(bring_kernel, name='bring', out_shape=(keys_shape, keys_sh...]
    all_gather x2 -> x0, blocking collectives: 177 us -> none  [the longest x1 136 us: on_device(): lax.all_gather(pooled_k, 'tok', axis=0, tiled=True)]
    all_to_all x13 -> x0, waiting for transfers between devices: 157 us -> none  [the longest x1 114 us: on_device(): lax.all_to_all(packed_keys, 'tok', split_axis=0, concat_axis=0, tiled=True)]
    all_to_all x13 -> x0, starting transfers between devices: 75.4 us -> none  [the longest x1 17.4 us: on_device(): lax.all_to_all(packed_keys, 'tok', split_axis=0, concat_axis=0, tiled=True)]
    scatter-add x10 -> x0, other arithmetic: 75.3 us -> none  [the longest x5 37.7 us: on_device(): jax.ops.segment_sum(grad_key.reshape(cubes_dev * topk, cube * hdim), slot...]
    dot_general x34 -> x0, matrix products: 73.8 us -> none  [the longest x6 31.1 us: attend_back(): jnp.einsum('tqk,tqd->tkd', probs_low, grad_rows, preferred_element_type=j...]
    gather x13 -> x0, local copies, waits for them, and re-layouts: 59 us -> none  [the longest x2 25.8 us: on_device(): chosen = jnp.take(tile_of_cube, listed, axis=0)]
  transfers between devices with their start and end apart: 14 -> 0, of which waited for: 9 -> 0; matrix products, arithmetic and copies ran while one was open for 25% -> 0% of each run, Pallas kernels for 0% -> 0%
where the time goes in v1:
time: 208 us; the launch traced here: 207 us
  Pallas kernels  197 us (95%)
  local copies, waits for them, and re-layouts  9.65 us (5%)
    pallas_call x1, Pallas kernels, bring(): pl.pallas_call(bring_kernel, name='bring', out_shape=(keys_shape, keys_sh...  85.9 us
    pallas_call x1, Pallas kernels, home(): pl.pallas_call(home_kernel, name='home', out_shape=(out_shape,) * 3, in_s...  76.7 us
    pallas_call x1, Pallas kernels, attend(): pl.pallas_call(attend_kernel, name='attend', out_shape=(query_shape, keys...  34.4 us
    unnamed x19, local copies, waits for them, and re-layouts  9.65 us

profile of v1, /device:TPU:1, one launch (start us, length us, event | category | flops | bytes accessed | tf_op | source)
XLA Modules:
  0.0 207.3 jit_solution(4254691552508073532)
XLA Ops:
  0.6 0.0 copy-start
  0.6 1.1 copy-done
  1.7 0.0 copy-start.1
  1.7 1.1 copy-done.1
  2.8 0.0 copy-start.2
  2.8 1.1 copy-done.2
  3.9 0.0 copy-start.3
  3.9 1.1 copy-done.3
  5.0 0.0 copy-start.5
  5.0 0.7 copy-done.5
  5.7 0.0 copy-start.6
  5.7 0.7 copy-done.6
  6.4 85.9 %bring.1 = (bf16[32,8,64,128]{3,2,1,0:T(8,128)(2,1)S(1)}, bf16[32,8,64,128]{3,2,1,0:T(8,128)(2,1)S(1)}, bf16[6,8,64,128]{3,2,1,0:T(8,128)(2,1)S(1)}, bf16[6,8,64...) custom-call(bf16[64,5120]{1,0:T(8,128)(2,1)S(1)} %copy-done, bf16[64,5120]{1,0:T(8,128)(2,1)S(1)} %copy-done.1, ...), custom_call_target="tpu_custom_call" | custom-call | tf_op jit(solution)/shard_map/bring/pallas_call | solution.py:274
  92.3 0.0 copy-start.4
  92.3 0.7 copy-done.4
  93.0 0.0 copy-start.7
  93.0 0.7 copy-done.7
  93.7 34.4 %attend.1 = (bf16[48,64,128]{2,1,0:T(8,128)(2,1)S(1)}, bf16[256,64,128]{2,1,0:T(8,128)(2,1)S(1)}, bf16[256,64,128]{2,1,0:T(8,128)(2,1)S(1)}) custom-call(s32[256]{0:T(256)S(1)} %copy-done.7, s32[16,256]{1,0:T(8,128)S(1)} %bitcast.19, bf16[48,64,128]{2,1,0:T(8,128)(2,1)S(1)} %bitcast.16, bf16[48,64,128]{2,1,0:T(8,128)(2,1)S(1)} %bitcast.17, ...), custom_call_target="tpu_custom_call" | custom-call | tf_op jit(solution)/shard_map/attend/pallas_call | solution.py:439
  128.1 76.7 %home.1 = (bf16[64,5120]{1,0:T(8,128)(2,1)S(1)}, bf16[64,5120]{1,0:T(8,128)(2,1)S(1)}, bf16[64,5120]{1,0:T(8,128)(2,1)S(1)}) custom-call(bf16[6,8,64,128]{3,2,1,0:T(8,128)(2,1)S(1)} %bitcast.15, bf16[32,8,64,128]{3,2,1,0:T(8,128)(2,1)S(1)} %bitcast.11, bf16[32,8,64,128]{3,2,1,0:T(8,128)(2,1)S(1)} %bitcast.12), custom_call_target="tpu_custom_call" | custom-call | tf_op jit(solution)/shard_map/home/pallas_call | solution.py:618
  204.8 0.8 copy.14
  205.6 0.8 copy.15
  206.4 0.8 copy.16
Async XLA Ops:
  0.6 1.1 copy-start
  1.7 1.1 copy-start.1
  2.8 1.1 copy-start.2
  3.9 1.1 copy-start.3
  5.0 0.7 copy-start.5
  5.7 0.7 copy-start.6
  92.3 0.7 copy-start.4
  93.0 0.7 copy-start.7

commit v2 on v1

--- a/solution.py
+++ b/solution.py
@@ -28,6 +28,7 @@
 STAGES = 8
 ATTEND_VMEM = 30 * 2**20
 HOME_VMEM = 20 * 2**20
+BRING_VMEM = 16 * 2**20
 
 
 def where_am_i():
@@ -89,14 +90,12 @@
 
 
 def bring_kernel(
-    k_in, v_in, q_in, g_hbm, fgate, cgate,
+    k_in, v_in, q_in, g_in, fgate, cgate,
     kh, vh, qh, fh, ph,
-    kz, vz, qz, fz, pz, fg, pg, g_in,
-    gsem, zsend, zrecv, psend, krecv, qrecv, fsend, frecv,
+    packed, kz, vz, qz, fz, pz, pg,
+    zsend, zrecv, psend, krecv, qrecv, fsend, frecv,
 ):
     plane, chip, core = where_am_i()
-    load_grad = pltpu.make_async_copy(g_hbm, g_in, gsem)
-    load_grad.start()
     greet(plane, chip, core)
 
     def start_along_z(stage, source, landing):
@@ -111,24 +110,30 @@
         lax.fori_loop(1, PLANES, step, 0)
         pltpu.make_async_copy(source(plane), landing(plane), zrecv.at[stage]).start()
 
-    sources = (
-        lambda t, rows: k_in.at[rows, columns(t)],
-        lambda t, rows: v_in.at[rows, columns(t)],
-        lambda t, rows: q_in.at[rows, columns(t)],
-        lambda t, rows: fg.at[t, rows],
-    )
     slabs = (kz, vz, qz, fz)
     outs = (kh, vh, qh, fh)
 
     def start_stage(stage):
         number, rows = stage // 2, rows_of(stage % 2)
         start_along_z(
-            stage, lambda t: sources[number](t, rows), lambda t: slabs[number].at[t, rows]
+            stage,
+            lambda t: packed.at[number, t, :, rows],
+            lambda t: slabs[number].at[:, t, rows],
         )
 
+    def pack(number, source):
+        def step(group, _):
+            for j in range(HEADS_PLANE):
+                packed[number, group, j] = source[:, columns(group * HEADS_PLANE + j, HDIM)]
+            return 0
+
+        lax.fori_loop(0, PLANES, step, 0)
+
+    pack(0, k_in)
     start_stage(0)
     start_stage(1)
-    load_grad.wait()
+    pack(1, v_in)
+    pack(2, q_in)
 
     def gates(group, _):
         row = lax.broadcasted_iota(jnp.int32, (fgate.shape[0], WIDTH), 0)
@@ -137,11 +142,13 @@
             row == group * HEADS_PLANE + lax.shift_right_logical(col, 7), 1.0, 0.0
         ).astype(BF16)
         grad = g_in[:, columns(group)].astype(F32)
-        fine = tn(fgate[...], spread)
-        fg[group] = (fine * grad).astype(BF16)
+        fine = (tn(fgate[...], spread) * grad).astype(BF16)
         coarse = tn(cgate[...], spread)
         pooled = jnp.sum(coarse * grad, axis=0, keepdims=True)
-        rows = [pooled[:, j * HDIM:(j + 1) * HDIM] for j in range(HEADS_PLANE)]
+        rows = []
+        for j in range(HEADS_PLANE):
+            packed[3, group, j] = fine[:, j * HDIM:(j + 1) * HDIM]
+            rows.append(pooled[:, j * HDIM:(j + 1) * HDIM])
         rows.append(jnp.zeros((16 - HEADS_PLANE, HDIM), F32))
         pg[group] = jnp.concatenate(rows, axis=0).astype(BF16)
         return 0
@@ -157,7 +164,7 @@
             @pl.when(target < WORKERS)
             def _():
                 remote(
-                    landed.at[:, rows, columns(head_of(target), HDIM)],
+                    landed.at[head_of(target), :, rows],
                     out.at[core * CHIPS + chip, :, rows],
                     psend.at[number], krecv.at[number, chip], device_of(plane, target, core),
                 ).start()
@@ -169,7 +176,7 @@
         @pl.when(chip < WORKERS)
         def _():
             pltpu.make_async_copy(
-                landed.at[:, rows, columns(head_of(chip), HDIM)],
+                landed.at[head_of(chip), :, rows],
                 out.at[core * CHIPS + chip, :, rows],
                 krecv.at[number, chip],
             ).start()
@@ -197,7 +204,7 @@
 
     for stage in range(STAGES):
         number, rows = stage // 2, rows_of(stage % 2)
-        take_bytes(slabs[number].at[:, rows], zrecv.at[stage])
+        take_bytes(slabs[number].at[:, :, rows], zrecv.at[stage])
         if stage + 2 < STAGES:
             start_stage(stage + 2)
         if stage + 2 == STAGES:
@@ -207,7 +214,7 @@
         else:
             share_queries(
                 number,
-                lambda j, number=number, rows=rows: slabs[number].at[:, rows, columns(j, HDIM)],
+                lambda j, number=number, rows=rows: slabs[number].at[j, :, rows],
                 lambda i, number=number, rows=rows: outs[number].at[i, :, rows],
             )
     take_bytes(pz, zrecv.at[STAGES])
@@ -243,7 +250,7 @@
             take_bytes(theirs, fsend.at[number])
 
     for stage in range(STAGES):
-        landed = slabs[stage // 2].at[pl.ds(0, PLANES - 1), rows_of(stage % 2)]
+        landed = slabs[stage // 2].at[:, pl.ds(0, PLANES - 1), rows_of(stage % 2)]
         take_bytes(landed, zsend.at[stage])
     take_bytes(pz.at[pl.ds(0, PLANES - 1)], zsend.at[STAGES])
 
@@ -267,20 +274,18 @@
     query_shape = jax.ShapeDtypeStruct((QGROUPS, PLANES, CUBE, HDIM), BF16)
     pooled_shape = jax.ShapeDtypeStruct((QGROUPS, PLANES, 16, HDIM), BF16)
     anywhere = pl.BlockSpec(memory_space=pl.ANY)
-    in_hbm = pl.BlockSpec(memory_space=pltpu.HBM)
     in_vmem = pl.BlockSpec(memory_space=pltpu.VMEM)
-    slab = pltpu.VMEM((PLANES, CUBE, WIDTH), BF16)
+    slab = pltpu.VMEM((HEADS_PLANE, PLANES, CUBE, HDIM), BF16)
     small = pltpu.VMEM((PLANES, 16, HDIM), BF16)
     return pl.pallas_call(
         bring_kernel,
         name="bring",
         out_shape=(keys_shape, keys_shape, query_shape, query_shape, pooled_shape),
-        in_specs=[in_hbm] * 4 + [in_vmem] * 2,
+        in_specs=[in_vmem] * 6,
         out_specs=[anywhere] * 5,
         scratch_shapes=[
-            slab, slab, slab, slab, small, slab, small,
-            pltpu.VMEM(grad_out.shape, BF16),
-            pltpu.SemaphoreType.DMA,
+            pltpu.VMEM((4, PLANES, HEADS_PLANE, CUBE, HDIM), BF16),
+            slab, slab, slab, slab, small, small,
             pltpu.SemaphoreType.DMA((STAGES + 1,)),
             pltpu.SemaphoreType.DMA((STAGES + 1,)),
             pltpu.SemaphoreType.DMA((5,)),
@@ -290,7 +295,7 @@
             pltpu.SemaphoreType.DMA((2,)),
         ],
         compiler_params=pltpu.CompilerParams(
-            collective_id=0, has_side_effects=True, vmem_limit_bytes=16 * 2**20
+            collective_id=0, has_side_effects=True, vmem_limit_bytes=BRING_VMEM
         ),
     )(keys_in, values, queries, grad_out, fine_gate.T, coarse_gate.T)
 
@@ -464,7 +469,7 @@
 def home_kernel(
     dq, dk, dv,
     oq, ok, ov,
-    own_k, own_v, sib_k, sib_v, land_q, land_k, land_v, sum_k, sum_v,
+    own_k, own_v, sib_k, sib_v, land_q, land_k, land_v, sum_k, sum_v, sum_q,
     ssend, srecv, psend, precv, zsend, zrecv,
 ):
     plane, chip, core = where_am_i()
@@ -474,7 +479,6 @@
     sibling = device_of(plane, chip, 1 - core)
     sources, owns, sibs = (dk, dv), (own_k, own_v), (sib_k, sib_v)
     lands, sums, outs = (land_k, land_v), (sum_k, sum_v), (ok, ov)
-    spread = columns(head, HDIM)
     mine = columns(plane)
 
     @pl.when(works)
@@ -497,13 +501,13 @@
             @pl.when((wanted < CHIPS) & (target != chip))
             def _():
                 remote(
-                    dq.at[i], land_q.at[:, :, spread], psend.at[2], precv.at[4],
+                    dq.at[i], land_q.at[head], psend.at[2], precv.at[4],
                     device_of(plane, target, core),
                 ).start()
 
             @pl.when(wanted == chip)
             def _():
-                pltpu.make_async_copy(dq.at[i], land_q.at[:, :, spread], precv.at[4]).start()
+                pltpu.make_async_copy(dq.at[i], land_q.at[head], precv.at[4]).start()
 
             return 0
 
@@ -526,14 +530,14 @@
             @pl.when(target != chip)
             def _():
                 remote(
-                    own.at[target, :, rows], land.at[replica, :, rows, spread], psend.at[number],
+                    own.at[target, :, rows], land.at[replica, head, :, rows], psend.at[number],
                     arrived, device_of(plane, target, core),
                 ).start()
 
             @pl.when(target == chip)
             def _():
                 pltpu.make_async_copy(
-                    own.at[target, :, rows], land.at[replica, :, rows, spread], arrived
+                    own.at[target, :, rows], land.at[replica, head, :, rows], arrived
                 ).start()
 
             return 0
@@ -558,7 +562,9 @@
 
         def step(d, _):
             target = (plane + d) % PLANES
-            send_home(2, land_q.at[target], oq.at[:, mine], target)
+            for j in range(HEADS_PLANE):
+                sum_q[target, :, j * HDIM:(j + 1) * HDIM] = land_q[j, target]
+            send_home(2, sum_q.at[target], oq.at[:, mine], target)
             return 0
 
         lax.fori_loop(0, PLANES, step, 0)
@@ -566,14 +572,15 @@
     def keys_home(number, half):
         rows = rows_of(half)
         land, total, out = lands[number], sums[number], outs[number]
-        take_bytes(land.at[:, :, rows], precv.at[number * 2 + half])
+        take_bytes(land.at[:, :, :, rows], precv.at[number * 2 + half])
 
         def step(d, _):
             target = (plane + d) % PLANES
-            summed = land[0, target, rows].astype(F32)
-            for r in range(1, COPIES):
-                summed += land[r, target, rows].astype(F32)
-            total[target, rows] = summed.astype(BF16)
+            for j in range(HEADS_PLANE):
+                summed = land[0, j, target, rows].astype(F32)
+                for r in range(1, COPIES):
+                    summed += land[r, j, target, rows].astype(F32)
+                total[target, rows, j * HDIM:(j + 1) * HDIM] = summed.astype(BF16)
             send_home(number, total.at[target, rows], out.at[rows, mine], target)
             return 0
 
@@ -591,7 +598,7 @@
 
     for number, out in enumerate((ok, ov, oq)):
         take_bytes(out, zrecv.at[number])
-        take_bytes(land_q.at[pl.ds(0, PLANES - 1)], zsend.at[number])
+        take_bytes(sum_q.at[pl.ds(0, PLANES - 1)], zsend.at[number])
 
     @pl.when(works)
     def _():
@@ -614,7 +621,8 @@
     out_shape = jax.ShapeDtypeStruct((rows, width), BF16)
     half = pltpu.VMEM((CHIPS, PLANES, CUBE, HDIM), BF16)
     slab = pltpu.VMEM((PLANES, CUBE, WIDTH), BF16)
-    slabs = pltpu.VMEM((COPIES, PLANES, CUBE, WIDTH), BF16)
+    by_head = pltpu.VMEM((HEADS_PLANE, PLANES, CUBE, HDIM), BF16)
+    copies = pltpu.VMEM((COPIES, HEADS_PLANE, PLANES, CUBE, HDIM), BF16)
     return pl.pallas_call(
         home_kernel,
         name="home",
@@ -622,7 +630,7 @@
         in_specs=[anywhere, in_vmem, in_vmem],
         out_specs=[anywhere] * 3,
         scratch_shapes=[
-            half, half, half, half, slab, slabs, slabs, slab, slab,
+            half, half, half, half, by_head, copies, copies, slab, slab, slab,
             pltpu.SemaphoreType.DMA((2,)),
             pltpu.SemaphoreType.DMA((2, CHIPS)),
             pltpu.SemaphoreType.DMA((3,)),

time: 208 us -> 207 us (level)
  no operation moved by 1% of the time
where the time goes in v2:
time: 207 us; the launch traced here: 205 us
  Pallas kernels  195 us (94%)
  local copies, waits for them, and re-layouts  9.65 us (5%)
    pallas_call x1, Pallas kernels, bring(): pl.pallas_call(bring_kernel, name='bring', out_shape=(keys_shape, keys_sh...  84.2 us
    pallas_call x1, Pallas kernels, home(): pl.pallas_call(home_kernel, name='home', out_shape=(out_shape,) * 3, in_s...  75.9 us
    pallas_call x1, Pallas kernels, attend(): pl.pallas_call(attend_kernel, name='attend', out_shape=(query_shape, keys...  34.4 us
    unnamed x19, local copies, waits for them, and re-layouts  9.65 us

profile of v2, /device:TPU:1, one launch (start us, length us, event | category | flops | bytes accessed | tf_op | source)
XLA Modules:
  0.0 204.8 jit_solution(17474032276472688208)
XLA Ops:
  0.6 0.0 copy-start
  0.6 1.1 copy-done
  1.7 0.0 copy-start.1
  1.7 1.1 copy-done.1
  2.8 0.0 copy-start.2
  2.8 1.1 copy-done.2
  3.9 0.0 copy-start.3
  3.9 1.1 copy-done.3
  5.0 0.0 copy-start.5
  5.0 0.7 copy-done.5
  5.7 0.0 copy-start.6
  5.7 0.7 copy-done.6
  6.4 84.2 %bring.1 = (bf16[32,8,64,128]{3,2,1,0:T(8,128)(2,1)S(1)}, bf16[32,8,64,128]{3,2,1,0:T(8,128)(2,1)S(1)}, bf16[6,8,64,128]{3,2,1,0:T(8,128)(2,1)S(1)}, bf16[6,8,64...) custom-call(bf16[64,5120]{1,0:T(8,128)(2,1)S(1)} %copy-done, bf16[64,5120]{1,0:T(8,128)(2,1)S(1)} %copy-done.1, ...), custom_call_target="tpu_custom_call" | custom-call | tf_op jit(solution)/shard_map/bring/pallas_call | solution.py:280
  90.6 0.0 copy-start.4
  90.6 0.7 copy-done.4
  91.3 0.0 copy-start.7
  91.3 0.7 copy-done.7
  92.0 34.4 %attend.1 = (bf16[48,64,128]{2,1,0:T(8,128)(2,1)S(1)}, bf16[256,64,128]{2,1,0:T(8,128)(2,1)S(1)}, bf16[256,64,128]{2,1,0:T(8,128)(2,1)S(1)}) custom-call(s32[256]{0:T(256)S(1)} %copy-done.7, s32[16,256]{1,0:T(8,128)S(1)} %bitcast.19, bf16[48,64,128]{2,1,0:T(8,128)(2,1)S(1)} %bitcast.16, bf16[48,64,128]{2,1,0:T(8,128)(2,1)S(1)} %bitcast.17, ...), custom_call_target="tpu_custom_call" | custom-call | tf_op jit(solution)/shard_map/attend/pallas_call | solution.py:444
  126.4 75.9 %home.1 = (bf16[64,5120]{1,0:T(8,128)(2,1)S(1)}, bf16[64,5120]{1,0:T(8,128)(2,1)S(1)}, bf16[64,5120]{1,0:T(8,128)(2,1)S(1)}) custom-call(bf16[6,8,64,128]{3,2,1,0:T(8,128)(2,1)S(1)} %bitcast.15, bf16[32,8,64,128]{3,2,1,0:T(8,128)(2,1)S(1)} %bitcast.11, bf16[32,8,64,128]{3,2,1,0:T(8,128)(2,1)S(1)} %bitcast.12), custom_call_target="tpu_custom_call" | custom-call | tf_op jit(solution)/shard_map/home/pallas_call | solution.py:626
  202.3 0.8 copy.14
  203.2 0.8 copy.15
  204.0 0.8 copy.16
Async XLA Ops:
  0.6 1.1 copy-start
  1.7 1.1 copy-start.1
  2.8 1.1 copy-start.2
  3.9 1.1 copy-start.3
  5.0 0.7 copy-start.5
  5.7 0.7 copy-start.6
  90.6 0.7 copy-start.4
  91.3 0.7 copy-start.7

commit v3 on v2

v3 whole, which is shorter than its diff:
```python
import functools
import math

import jax
import jax.numpy as jnp
from jax import lax
from jax.experimental import pallas as pl
from jax.experimental.pallas import tpu as pltpu
from jax.sharding import PartitionSpec as P

MESH = pl.DeviceIdType.MESH
BF16 = jnp.bfloat16
F32 = jnp.float32

CUBE = 64
HDIM = 128
PLANES = 8
CHIPS = 16
SIDE = 4
HEADS_PLANE = 5
COPIES = 3
WORKERS = HEADS_PLANE * COPIES
WIDTH = HEADS_PLANE * HDIM
QGROUPS = 6
TOPK = 16
SLOTS = 2 * CHIPS * PLANES
UNITS = QGROUPS * PLANES
HALF = CUBE // 2
STAGES = 8
HOPS = ((), (), ((0, 0),), ((0, 1),), ((0, 2), (1, 0)), ((0, 3), (1, 1)), ((1, 2),), ((1, 3),))
ALL = slice(None)
EXTRA = ((0, 4), (4, 2), (6, 2))
ATTEND_VMEM = 30 * 2**20
HOME_VMEM = 26 * 2**20
BRING_VMEM = 16 * 2**20


def where_am_i():
    tok = lax.axis_index("tok")
    head = lax.axis_index("head")
    plane = tok // 4
    chip = (tok // 2) % 2 * 8 + head
    core = tok % 2
    return plane, chip, core


def place_of(chip):
    x, y = chip % SIDE, chip // SIDE
    in_row = x < COPIES
    return x, y, in_row, jnp.where(in_row, x, y), jnp.where(in_row, y, HEADS_PLANE - 1)


def on_line(x, y, at):
    return jnp.where(x < COPIES, y * SIDE + at, at * SIDE + COPIES)


def source_of(group, x, y):
    in_row = jnp.where(group < SIDE, group * SIDE + x, x * SIDE + COPIES)
    in_column = jnp.where(group < SIDE, y * SIDE + group, COPIES * SIDE + y)
    return jnp.where(group < SIDE + 1, jnp.where(x < COPIES, in_row, in_column), WORKERS)


def device_of(plane, chip, core):
    return {"tok": plane * 4 + chip // 8 * 2 + core, "head": chip % 8}


def remote(src, dst, send, recv, device):
    return pltpu.make_async_remote_copy(
        src_ref=src, dst_ref=dst, send_sem=send, recv_sem=recv, device_id=device, device_id_type=MESH
    )


def take_bytes(ref, sem):
    pltpu.make_async_copy(ref, ref, sem).wait()


def greet(plane, chip, core):
    barrier = pltpu.get_barrier_semaphore()

    def along_z(d, _):
        pl.semaphore_signal(
            barrier, inc=1, device_id=device_of((plane + d) % PLANES, chip, core), device_id_type=MESH
        )
        return 0

    def in_plane(d, _):
        pl.semaphore_signal(
            barrier, inc=1, device_id=device_of(plane, (chip + d) % CHIPS, core), device_id_type=MESH
        )
        return 0

    lax.fori_loop(1, PLANES, along_z, 0)
    lax.fori_loop(1, CHIPS, in_plane, 0)
    pl.semaphore_signal(
        barrier, inc=1, device_id=device_of(plane, chip, 1 - core), device_id_type=MESH
    )
    pl.semaphore_wait(barrier, PLANES - 1 + CHIPS - 1 + 1)


def columns(group, width=WIDTH):
    return pl.ds(pl.multiple_of(group * width, 128), width)


def rows_of(half):
    return pl.ds(half * HALF, HALF)


def bring_kernel(
    k_in, v_in, q_in, g_in, fgate, cgate,
    kh, vh, qh, fh, ph,
    packed, kz, vz, qz, fz, pz, pg,
    zsend, zrecv, ysend, lsend, psend, krecv, qrecv, xrecv, fsend, frecv,
):
    plane, chip, core = where_am_i()
    greet(plane, chip, core)

    def start_along_z(stage, source, landing):
        def step(d, _):
            target = (plane + d) % PLANES
            remote(
                source(target), landing(plane), zsend.at[stage], zrecv.at[stage],
                device_of(target, chip, core),
            ).start()
            return 0

        lax.fori_loop(1, PLANES, step, 0)
        pltpu.make_async_copy(source(plane), landing(plane), zrecv.at[stage]).start()

    x, y, in_row, spot, _ = place_of(chip)
    works = chip < WORKERS
    slabs = (kz, vz, qz, fz)
    outs = (kh, vh, qh, fh)

    def start_stage(stage):
        number, rows = stage // 2, rows_of(stage % 2)
        start_along_z(
            stage,
            lambda t: packed.at[number, t, :, rows],
            lambda t: slabs[number].at[:, t, rows],
        )

    def pack(number, source):
        def step(group, _):
            for j in range(HEADS_PLANE):
                packed[number, group, j] = source[:, columns(group * HEADS_PLANE + j, HDIM)]
            return 0

        lax.fori_loop(0, PLANES, step, 0)

    pack(0, k_in)
    start_stage(0)
    start_stage(1)
    pack(1, v_in)
    pack(2, q_in)

    def gates(group, _):
        row = lax.broadcasted_iota(jnp.int32, (fgate.shape[0], WIDTH), 0)
        col = lax.broadcasted_iota(jnp.int32, (fgate.shape[0], WIDTH), 1)
        spread = jnp.where(
            row == group * HEADS_PLANE + lax.shift_right_logical(col, 7), 1.0, 0.0
        ).astype(BF16)
        grad = g_in[:, columns(group)].astype(F32)
        fine = (tn(fgate[...], spread) * grad).astype(BF16)
        coarse = tn(cgate[...], spread)
        pooled = jnp.sum(coarse * grad, axis=0, keepdims=True)
        rows = []
        for j in range(HEADS_PLANE):
            packed[3, group, j] = fine[:, j * HDIM:(j + 1) * HDIM]
            rows.append(pooled[:, j * HDIM:(j + 1) * HDIM])
        rows.append(jnp.zeros((16 - HEADS_PLANE, HDIM), F32))
        pg[group] = jnp.concatenate(rows, axis=0).astype(BF16)
        return 0

    lax.fori_loop(0, PLANES, gates, 0)

    def share_keys(number, rows):
        landed, out = slabs[number], outs[number]

        def step(j, _):
            row_head = j < SIDE
            target = jnp.where(row_head, j * SIDE + x, y * SIDE + COPIES)
            piece = jnp.where(row_head, x * SIDE + y, y * SIDE + x)
            aside = (row_head & (x == COPIES)).astype(jnp.int32)
            region = jnp.where(aside == 1, 2, core)
            here, there = landed.at[j, :, rows], out.at[region, piece, :, rows]
            arrived = krecv.at[number, aside, piece]

            @pl.when(target != chip)
            def _():
                remote(
                    here, there, ysend.at[number], arrived, device_of(plane, target, core)
                ).start()

            @pl.when(target == chip)
            def _():
                pltpu.make_async_copy(here, there, arrived).start()

            return 0

        lax.fori_loop(0, HEADS_PLANE, step, 0)

    def pass_on(number, hop):
        out = outs[number]

        def step(s, _):
            turn = s // 2
            way, stop = 1 - 2 * turn, 2 - 2 * turn

            def role(aside, region, at, target_of):
                piece = (at + 8 - way * hop) % SIDE * SIDE + s
                block = out.at[region, piece]
                after = (at + SIDE + way) % SIDE

                @pl.when((at != COPIES) | (hop < 3))
                def _():
                    take_bytes(block, krecv.at[number, aside, piece])

                if hop < 3:
                    to_side = (in_row & (after == COPIES)).astype(jnp.int32)

                    @pl.when((at != stop) | (hop < 2))
                    def _():
                        remote(
                            block, out.at[jnp.where(to_side == 1, 2, core), piece],
                            lsend.at[number, aside], krecv.at[number, to_side, piece],
                            device_of(plane, target_of(after), core),
                        ).start()

                if aside == 0:
                    @pl.when(works)
                    def _():
                        remote(
                            block, block, fsend.at[number], frecv.at[number],
                            device_of(plane, chip, 1 - core),
                        ).start()

            role(0, core, spot, lambda after: on_line(x, y, after))

            @pl.when(x == COPIES)
            def _():
                role(1, 2, jnp.int32(COPIES), lambda after: y * SIDE + after)

            return 0

        lax.fori_loop(0, SIDE, step, 0)

    def share_queries(number, pick, place):
        def step(j, _):
            row_head = j < SIDE
            at, source = jnp.where(row_head, x, y), jnp.where(row_head, y, x)
            line = lambda to: jnp.where(row_head, j * SIDE + to, to * SIDE + COPIES)
            direct = at < COPIES
            target = line(jnp.where(direct, at, jnp.minimum(source, COPIES - 1)))
            group = jnp.where(direct, source, SIDE)

            @pl.when(works & (target != chip))
            def _():
                remote(
                    pick(j, ALL), place(group, ALL), psend.at[number],
                    qrecv.at[number - 2], device_of(plane, target, core),
                ).start()

            @pl.when(works & (target == chip))
            def _():
                pltpu.make_async_copy(
                    pick(j, ALL), place(group, ALL), qrecv.at[number - 2]
                ).start()

            @pl.when(chip >= WORKERS)
            def _():
                for copy, (first, count) in enumerate(EXTRA):
                    remote(
                        pick(j, pl.ds(first, count)), place(QGROUPS - 1, pl.ds(0, count)),
                        psend.at[number], xrecv.at[number - 2],
                        device_of(plane, line(copy), core),
                    ).start()

            return 0

        lax.fori_loop(0, HEADS_PLANE, step, 0)

    for stage in range(STAGES):
        number, rows = stage // 2, rows_of(stage % 2)
        take_bytes(slabs[number].at[:, :, rows], zrecv.at[stage])
        if stage + 2 < STAGES:
            start_stage(stage + 2)
        if stage + 2 == STAGES:
            start_along_z(STAGES, lambda t: pg.at[t], lambda t: pz.at[t])
        if number < 2:
            share_keys(number, rows)
        else:
            share_queries(
                number,
                lambda j, z, number=number, rows=rows: slabs[number].at[j, z, rows],
                lambda i, z, number=number, rows=rows: outs[number].at[i, z, rows],
            )
        for number, hop in HOPS[stage]:
            pass_on(number, hop)
    take_bytes(pz, zrecv.at[STAGES])
    share_queries(4, lambda j, z: pz.at[z], lambda i, z: ph.at[i, z])

    @pl.when(works)
    def _():
        for number, out in enumerate((qh, fh, ph)):
            take_bytes(out.at[pl.ds(0, QGROUPS - 1)], qrecv.at[number])
        for copy, (first, count) in enumerate(EXTRA):
            @pl.when(spot == copy)
            def _(count=count):
                for number, out in enumerate((qh, fh, ph)):
                    take_bytes(out.at[QGROUPS - 1, pl.ds(0, count)], xrecv.at[number])

        for number, out in ((0, kh), (1, vh)):
            take_bytes(out.at[1 - core], frecv.at[number])
            take_bytes(out.at[1 - core], fsend.at[number])
        for number, out in ((2, qh), (3, fh), (4, ph)):
            take_bytes(out.at[pl.ds(0, HEADS_PLANE - 1)], psend.at[number])

    @pl.when(chip >= WORKERS)
    def _():
        for number, out in ((2, qh), (3, fh), (4, ph)):
            take_bytes(out.at[pl.ds(0, HEADS_PLANE)], psend.at[number])

    for number, out in ((0, kh), (1, vh)):
        @pl.when(in_row)
        def _(number=number, out=out):
            take_bytes(out.at[0, pl.ds(0, 4)], ysend.at[number])

        @pl.when(x == COPIES)
        def _(number=number, out=out):
            take_bytes(out.at[0, pl.ds(0, 3)], ysend.at[number])
            take_bytes(out.at[0, pl.ds(0, 12)], lsend.at[number, 1])

        @pl.when(spot % 2 == 0)
        def _(number=number, out=out):
            take_bytes(out.at[0, pl.ds(0, 10)], lsend.at[number, 0])

        @pl.when(spot % 2 == 1)
        def _(number=number, out=out):
            take_bytes(out.at[0, pl.ds(0, 12)], lsend.at[number, 0])

    for stage in range(STAGES):
        landed = slabs[stage // 2].at[:, pl.ds(0, PLANES - 1), rows_of(stage % 2)]
        take_bytes(landed, zsend.at[stage])
    take_bytes(pz.at[pl.ds(0, PLANES - 1)], zsend.at[STAGES])


def bring(keys_in, values, queries, grad_out, fine_gate, coarse_gate):
    keys_shape = jax.ShapeDtypeStruct((3, CHIPS, PLANES, CUBE, HDIM), BF16)
    query_shape = jax.ShapeDtypeStruct((QGROUPS, PLANES, CUBE, HDIM), BF16)
    pooled_shape = jax.ShapeDtypeStruct((QGROUPS, PLANES, 16, HDIM), BF16)
    anywhere = pl.BlockSpec(memory_space=pl.ANY)
    in_vmem = pl.BlockSpec(memory_space=pltpu.VMEM)
    slab = pltpu.VMEM((HEADS_PLANE, PLANES, CUBE, HDIM), BF16)
    small = pltpu.VMEM((PLANES, 16, HDIM), BF16)
    return pl.pallas_call(
        bring_kernel,
        name="bring",
        out_shape=(keys_shape, keys_shape, query_shape, query_shape, pooled_shape),
        in_specs=[in_vmem] * 6,
        out_specs=[anywhere] * 5,
        scratch_shapes=[
            pltpu.VMEM((4, PLANES, HEADS_PLANE, CUBE, HDIM), BF16),
            slab, slab, slab, slab, small, small,
            pltpu.SemaphoreType.DMA((STAGES + 1,)),
            pltpu.SemaphoreType.DMA((STAGES + 1,)),
            pltpu.SemaphoreType.DMA((2,)),
            pltpu.SemaphoreType.DMA((2, 2)),
            pltpu.SemaphoreType.DMA((5,)),
            pltpu.SemaphoreType.DMA((2, 2, CHIPS)),
            pltpu.SemaphoreType.DMA((3,)),
            pltpu.SemaphoreType.DMA((3,)),
            pltpu.SemaphoreType.DMA((2,)),
            pltpu.SemaphoreType.DMA((2,)),
        ],
        compiler_params=pltpu.CompilerParams(
            collective_id=0, has_side_effects=True, vmem_limit_bytes=BRING_VMEM
        ),
    )(keys_in, values, queries, grad_out, fine_gate.T, coarse_gate.T)


def nt(a, b):
    return lax.dot_general(a, b, (((1,), (1,)), ((), ())), preferred_element_type=F32)


def tn(a, b):
    return lax.dot_general(a, b, (((0,), (0,)), ((), ())), preferred_element_type=F32)


def nn(a, b):
    return jnp.dot(a, b, preferred_element_type=F32)


def attend_kernel(
    toc, sel, q, fg, pg, k, v,
    dq, dk, dv,
    acc, wide, pk, pv, pq, cdq, part_k, part_v, cot, soc,
):
    _, chip, core = where_am_i()
    x, y, in_row, replica, head = place_of(chip)
    extra = jnp.where(replica == 0, EXTRA[0][1], EXTRA[1][1])
    skip = jnp.where(replica == 0, EXTRA[0][0], jnp.where(replica == 1, EXTRA[1][0], EXTRA[2][0]))
    units = jnp.where(chip < WORKERS, (QGROUPS - 1) * PLANES + extra, 0)
    factor = 1.0 / math.sqrt(HDIM)
    log2e = math.log2(math.e)

    def eighths(source, group):
        block = source[pl.ds(pl.multiple_of(group * 8, 8), 8)].astype(F32)
        return jnp.sum(block.reshape(8, 8, 8, HDIM), axis=1).reshape(64, HDIM)

    def prepare(group, _):
        rows = pl.ds(pl.multiple_of(group * 64, 64), 64)
        part_k[rows, :] = eighths(k, group)
        part_v[rows, :] = eighths(v, group)
        acc[pl.ds(pl.multiple_of(group * 8, 8), 8)] = jnp.zeros((8, CUBE, 2 * HDIM), F32)
        for i in range(8):
            cube = group * 8 + i
            tile = toc[cube]
            cot[tile] = cube
            at_x = tile & 3
            at_y = (lax.shift_right_logical(tile, 3) & 2) + (lax.shift_right_logical(tile, 2) & 1)
            piece = jnp.where(in_row, at_x * SIDE + at_y, at_y * SIDE + at_x)
            half = lax.shift_right_logical(tile, 3) & 1
            soc[cube] = (half * CHIPS + piece) * PLANES + lax.shift_right_logical(tile, 5)
        return 0

    lax.fori_loop(0, SLOTS // 8, prepare, 0)

    def pool(part, into):
        count = into.shape[0]
        total = part[pl.ds(0, count, stride=8), :]
        for row in range(1, 8):
            total += part[pl.ds(row, count, stride=8), :]
        into[...] = total * (1.0 / CUBE)

    pool(part_k, pk)
    pool(part_v, pv)

    def prepare_queries(group, _):
        part_k[pl.ds(pl.multiple_of(group * 64, 64), 64), :] = eighths(q, group)
        return 0

    lax.fori_loop(0, QGROUPS, prepare_queries, 0)
    pool(part_k, pq)
    unit_at = lax.broadcasted_iota(jnp.int32, (UNITS, 16, HDIM), 0)
    row_at = lax.broadcasted_iota(jnp.int32, (UNITS, 16, HDIM), 1)
    pooled_g = jnp.sum(
        jnp.where((unit_at < units) & (row_at == head), pg[...].astype(F32), 0.0), axis=1
    ).astype(BF16)
    live = lax.broadcasted_iota(jnp.int32, (UNITS, HDIM), 0) < units
    pooled_q = jnp.where(live, pq[...], 0.0).astype(BF16)
    pooled_k = pk[...].astype(BF16)
    pooled_v = pv[...].astype(BF16)
    scores = nt(pooled_q, pooled_k) * factor
    weights = jnp.exp(scores - jnp.max(scores, axis=1, keepdims=True))
    probs = weights / jnp.sum(weights, axis=1, keepdims=True)
    dprobs = nt(pooled_g, pooled_v)
    inner = jnp.sum(probs * dprobs, axis=1, keepdims=True)
    dscores = (probs * (dprobs - inner)).astype(BF16)
    cdq[...] = nn(dscores, pooled_k) * (factor / CUBE)
    pk[...] = tn(dscores, pooled_q) * (factor / CUBE)
    pv[...] = tn(probs.astype(BF16), pooled_g) * (1.0 / CUBE)
    wide[...] = jnp.zeros_like(wide)

    def listed(n):
        group, z = n // PLANES, n % PLANES
        origin = source_of(group, x, y)
        z = jnp.where(group == QGROUPS - 1, z + skip, z)
        tile = (z * 4 + origin // 8 * 2 + core) * 8 + origin % 8
        cube = cot[tile]
        slots = [soc[sel[r, cube]] for r in range(TOPK)]
        return [slots[c * 4:c * 4 + 4] for c in range(4)]

    def tiles_of(ref, quarter):
        return jnp.concatenate([ref[s] for s in quarter], axis=0)

    def softmax_terms(n, side, quarters):
        wide[side, :CUBE, :HDIM] = q[n]
        wide[side, CUBE:, HDIM:] = fg[n]
        both = [
            nt(wide[side], jnp.concatenate([tiles_of(k, quarter), tiles_of(v, quarter)], axis=1))
            for quarter in quarters
        ]
        score = [b[:CUBE] for b in both]
        dprob = [b[CUBE:] for b in both]
        top = functools.reduce(jnp.maximum, score)
        top = jnp.max(top, axis=1, keepdims=True)
        weight = [jnp.exp2((s - top) * (factor * log2e)) for s in score]
        total = jnp.sum(functools.reduce(jnp.add, weight), axis=1, keepdims=True)
        inverse = 1.0 / total
        mixed = functools.reduce(jnp.add, [w * d for w, d in zip(weight, dprob)])
        center = jnp.sum(mixed, axis=1, keepdims=True) * inverse
        probs = [w * inverse for w in weight]
        dscore = [(p * (d - center)).astype(BF16) for p, d in zip(probs, dprob)]
        return [p.astype(BF16) for p in probs], dscore

    def spread_terms(n, side, quarters, probs, dscore):
        dquery = jnp.zeros((CUBE, HDIM), F32)
        for c, quarter in enumerate(quarters):
            dquery += nn(dscore[c], tiles_of(k, quarter))
            terms = tn(jnp.concatenate([dscore[c], probs[c]], axis=0), wide[side])
            for i, s in enumerate(quarter):
                acc[s] += terms[i * CUBE:(i + 1) * CUBE]
        dq[n] = (dquery * factor + cdq[pl.ds(n, 1), :]).astype(BF16)

    def pair(m, _):
        numbers = [2 * m, 2 * m + 1]
        lists = [listed(n) for n in numbers]
        terms = [softmax_terms(n, i, quarters) for i, (n, quarters) in enumerate(zip(numbers, lists))]
        for i, (n, quarters, (probs, dscore)) in enumerate(zip(numbers, lists, terms)):
            spread_terms(n, i, quarters, probs, dscore)
        return 0

    lax.fori_loop(0, units // 2, pair, 0)

    def finish(group, _):
        for i in range(4):
            slot = group * 4 + i
            dk[slot] = (acc[slot, :, :HDIM] * factor + pk[pl.ds(slot, 1), :]).astype(BF16)
            dv[slot] = (acc[slot, :, HDIM:] + pv[pl.ds(slot, 1), :]).astype(BF16)
        return 0

    lax.fori_loop(0, SLOTS // 4, finish, 0)


def attend(tile_of_cube, select, qh, fh, ph, kh, vh):
    smem = pl.BlockSpec(memory_space=pltpu.SMEM)
    vmem = pl.BlockSpec(memory_space=pltpu.VMEM)
    query_shape = jax.ShapeDtypeStruct((UNITS, CUBE, HDIM), BF16)
    keys_shape = jax.ShapeDtypeStruct((SLOTS, CUBE, HDIM), BF16)
    return pl.pallas_call(
        attend_kernel,
        name="attend",
        out_shape=(query_shape, keys_shape, keys_shape),
        in_specs=[smem] * 2 + [vmem] * 5,
        out_specs=[vmem] * 3,
        scratch_shapes=[
            pltpu.VMEM((SLOTS, CUBE, 2 * HDIM), F32),
            pltpu.VMEM((2, 2 * CUBE, 2 * HDIM), BF16),
            pltpu.VMEM((SLOTS, HDIM), F32),
            pltpu.VMEM((SLOTS, HDIM), F32),
            pltpu.VMEM((UNITS, HDIM), F32),
            pltpu.VMEM((UNITS, HDIM), F32),
            pltpu.VMEM((SLOTS * 8, HDIM), F32),
            pltpu.VMEM((SLOTS * 8, HDIM), F32),
            pltpu.SMEM((SLOTS,), jnp.int32),
            pltpu.SMEM((SLOTS,), jnp.int32),
        ],
        compiler_params=pltpu.CompilerParams(vmem_limit_bytes=ATTEND_VMEM),
    )(
        tile_of_cube, select.T,
        qh.reshape(UNITS, CUBE, HDIM), fh.reshape(UNITS, CUBE, HDIM),
        ph.reshape(UNITS, 16, HDIM), kh.reshape(-1, CUBE, HDIM), vh.reshape(-1, CUBE, HDIM),
    )


def home_kernel(
    dq, dk, dv,
    oq, ok, ov,
    own_k, own_v, sib_k, sib_v, land_q, land_k, land_v, sum_k, sum_v, sum_q, chain_k, chain_v,
    ssend, srecv, psend, lsend, lrecv, ysend, precv, zsend, zrecv,
):
    plane, chip, core = where_am_i()
    x, y, in_row, spot, head = place_of(chip)
    works = chip < WORKERS
    greet(plane, chip, core)
    sources, owns, sibs, chains = (dk, dv), (own_k, own_v), (sib_k, sib_v), (chain_k, chain_v)
    lands, sums, outs = (land_k, land_v), (sum_k, sum_v), (ok, ov)
    mine = columns(plane)

    def turn_of(m):
        hop, s = m // SIDE, m % SIDE
        return hop, s, 1 - 2 * (s // 2), 2 - 2 * (s // 2)

    @pl.when(works)
    def _():
        def give(m, _):
            hop, s, way, _stop = turn_of(m)
            piece = (spot + 8 + way * (hop + 1)) % SIDE * SIDE + s
            for number in range(2):
                remote(
                    sources[number].at[(1 - core) * CHIPS + piece], sibs[number].at[piece],
                    ssend.at[number], srecv.at[number, piece],
                    device_of(plane, chip, 1 - core),
                ).start()
            return 0

        lax.fori_loop(0, CHIPS, give, 0)

        def send_query(i, _):
            target = source_of(i, x, y)

            @pl.when(target != chip)
            def _():
                remote(
                    dq.at[i], land_q.at[head], psend.at[0], precv.at[4],
                    device_of(plane, target, core),
                ).start()

            @pl.when(target == chip)
            def _():
                pltpu.make_async_copy(dq.at[i], land_q.at[head], precv.at[4]).start()

            return 0

        lax.fori_loop(0, QGROUPS - 1, send_query, 0)
        for copy, (first, count) in enumerate(EXTRA):
            @pl.when(spot == copy)
            def _(first=first, count=count):
                remote(
                    dq.at[QGROUPS - 1, pl.ds(0, count)], land_q.at[head, pl.ds(first, count)],
                    psend.at[1], precv.at[4], device_of(plane, CHIPS - 1, core),
                ).start()

    def gather(half):
        rows = rows_of(half)

        def step(m, _):
            hop, s, way, stop = turn_of(m)
            landing = jnp.minimum(hop, 2)
            arrival = jnp.maximum(hop - 1, 0)

            def deliver(number, block, at_x, at_y, to_head, aside):
                target = at_y * SIDE + at_x
                land, arrived = lands[number], precv.at[number * 2 + half]

                @pl.when(target != chip)
                def _():
                    remote(
                        block, land.at[to_head, :, rows], ysend.at[number, aside], arrived,
                        device_of(plane, target, core),
                    ).start()

                @pl.when(target == chip)
                def _():
                    pltpu.make_async_copy(block, land.at[to_head, :, rows], arrived).start()

            def hand_over(number, block, after, target, aside):
                to_side = (in_row & (after == COPIES)).astype(jnp.int32)
                remote(
                    block, chains[number].at[to_side, landing * SIDE + s, :, rows],
                    lsend.at[number, aside], lrecv.at[number, half, to_side, landing * SIDE + s],
                    device_of(plane, target, core),
                ).start()

            def relay(number, aside, target_of, at_x, at_y, to_head):
                block = chains[number].at[aside, arrival * SIDE + s, :, rows]
                after = (COPIES + SIDE - way) % SIDE

                @pl.when(hop > 0)
                def _():
                    take_bytes(block, lrecv.at[number, half, aside, arrival * SIDE + s])

                @pl.when((hop > 0) & (hop < 3))
                def _():
                    hand_over(number, block, after, target_of(after), aside)

                @pl.when(hop == 3)
                def _():
                    deliver(number, block, at_x, at_y, to_head, aside)

            for number in range(2):
                source, own, sib, chain = sources[number], owns[number], sibs[number], chains[number]

                @pl.when(works)
                def _(number=number, source=source, own=own, sib=sib, chain=chain):
                    piece = (spot + 8 + way * (hop + 1)) % SIDE * SIDE + s
                    if half == 0:
                        take_bytes(sib.at[piece], srecv.at[number, piece])
                    partial = lambda: (
                        source[core * CHIPS + piece, :, rows].astype(F32)
                        + sib[piece, :, rows].astype(F32)
                    )
                    fed = (hop > 1) | ((hop == 1) & (spot != stop))

                    @pl.when(fed)
                    def _():
                        came = chain.at[0, arrival * SIDE + s, :, rows]
                        take_bytes(came, lrecv.at[number, half, 0, arrival * SIDE + s])
                        own[piece, :, rows] = (partial() + came[...].astype(F32)).astype(BF16)

                    @pl.when(jnp.logical_not(fed))
                    def _():
                        own[piece, :, rows] = partial().astype(BF16)

                    block = own.at[piece, :, rows]
                    after = (spot + SIDE - way) % SIDE

                    @pl.when(hop < 3)
                    def _():
                        hand_over(number, block, after, on_line(x, y, after), 0)

                    @pl.when(hop == 3)
                    def _():
                        deliver(
                            number, block, jnp.where(in_row, x, s), jnp.where(in_row, s, y), head, 0
                        )

                @pl.when(chip >= WORKERS)
                def _(number=number):
                    relay(number, 0, lambda after: on_line(x, y, after), s, y, HEADS_PLANE - 1)

                @pl.when(x == COPIES)
                def _(number=number):
                    relay(number, 1, lambda after: y * SIDE + after, x, s, y)

            return 0

        lax.fori_loop(0, CHIPS, step, 0)

    def send_home(number, block, out, target):
        @pl.when(target != plane)
        def _():
            remote(
                block, out, zsend.at[number], zrecv.at[number], device_of(target, chip, core)
            ).start()

        @pl.when(target == plane)
        def _():
            pltpu.make_async_copy(block, out, zrecv.at[number]).start()

    def queries_home():
        take_bytes(land_q, precv.at[4])

        def step(d, _):
            target = (plane + d) % PLANES
            for j in range(HEADS_PLANE):
                sum_q[target, :, j * HDIM:(j + 1) * HDIM] = land_q[j, target]
            send_home(2, sum_q.at[target], oq.at[:, mine], target)
            return 0

        lax.fori_loop(0, PLANES, step, 0)

    def keys_home(number, half):
        rows = rows_of(half)
        land, total, out = lands[number], sums[number], outs[number]
        take_bytes(land.at[:, :, rows], precv.at[number * 2 + half])

        def step(d, _):
            target = (plane + d) % PLANES
            for j in range(HEADS_PLANE):
                total[target, rows, j * HDIM:(j + 1) * HDIM] = land[j, target, rows]
            send_home(number, total.at[target, rows], out.at[rows, mine], target)
            return 0

        lax.fori_loop(0, PLANES, step, 0)

    gather(0)
    queries_home()
    keys_home(0, 0)
    keys_home(1, 0)
    gather(1)
    keys_home(0, 1)
    keys_home(1, 1)

    for number, out in enumerate((ok, ov, oq)):
        take_bytes(out, zrecv.at[number])
        take_bytes(sum_q.at[pl.ds(0, PLANES - 1)], zsend.at[number])

    for number in range(2):
        own = owns[number]
        take_bytes(own.at[pl.ds(0, SIDE - 1)], ysend.at[number, 0])

        @pl.when(works)
        def _(number=number, own=own):
            take_bytes(sibs[number], ssend.at[number])
            take_bytes(own.at[pl.ds(0, 12)], lsend.at[number, 0])

        @pl.when(chip >= WORKERS)
        def _(number=number, own=own):
            take_bytes(own.at[pl.ds(0, 8)], lsend.at[number, 0])

        @pl.when(x == COPIES)
        def _(number=number, own=own):
            take_bytes(own.at[pl.ds(0, 8)], lsend.at[number, 1])
            take_bytes(own.at[pl.ds(0, SIDE - 1)], ysend.at[number, 1])

    @pl.when(works)
    def _():
        take_bytes(dq.at[pl.ds(0, QGROUPS - 2)], psend.at[0])
        for copy, (first, count) in enumerate(EXTRA):
            @pl.when(spot == copy)
            def _(count=count):
                take_bytes(dq.at[QGROUPS - 1, pl.ds(0, count)], psend.at[1])


def home(dq, dk, dv, rows, width):
    anywhere = pl.BlockSpec(memory_space=pl.ANY)
    in_vmem = pl.BlockSpec(memory_space=pltpu.VMEM)
    out_shape = jax.ShapeDtypeStruct((rows, width), BF16)
    half = pltpu.VMEM((CHIPS, PLANES, CUBE, HDIM), BF16)
    slab = pltpu.VMEM((PLANES, CUBE, WIDTH), BF16)
    by_head = pltpu.VMEM((HEADS_PLANE, PLANES, CUBE, HDIM), BF16)
    chain = pltpu.VMEM((2, 12, PLANES, CUBE, HDIM), BF16)
    return pl.pallas_call(
        home_kernel,
        name="home",
        out_shape=(out_shape,) * 3,
        in_specs=[anywhere, in_vmem, in_vmem],
        out_specs=[anywhere] * 3,
        scratch_shapes=[
            half, half, half, half, by_head, by_head, by_head, slab, slab, slab, chain, chain,
            pltpu.SemaphoreType.DMA((2,)),
            pltpu.SemaphoreType.DMA((2, CHIPS)),
            pltpu.SemaphoreType.DMA((2,)),
            pltpu.SemaphoreType.DMA((2, 2)),
            pltpu.SemaphoreType.DMA((2, 2, 2, 12)),
            pltpu.SemaphoreType.DMA((2, 2)),
            pltpu.SemaphoreType.DMA((5,)),
            pltpu.SemaphoreType.DMA((3,)),
            pltpu.SemaphoreType.DMA((3,)),
        ],
        compiler_params=pltpu.CompilerParams(
            collective_id=1, has_side_effects=True, vmem_limit_bytes=HOME_VMEM
        ),
    )(
        dq.reshape(QGROUPS, PLANES, CUBE, HDIM),
        dk.reshape(2 * CHIPS, PLANES, CUBE, HDIM),
        dv.reshape(2 * CHIPS, PLANES, CUBE, HDIM),
    )


def on_device(queries, keys_in, values, grad_out, fine_gate, coarse_gate, tile_of_cube, select):
    kh, vh, qh, fh, ph = bring(keys_in, values, queries, grad_out, fine_gate, coarse_gate)
    dq, dk, dv = attend(tile_of_cube, select, qh, fh, ph, kh, vh)
    return home(dq, dk, dv, *queries.shape)


def solution(mesh):
    split = P(("tok", "head"), None)
    return jax.shard_map(
        on_device,
        mesh=mesh,
        in_specs=(split,) * 6 + (P(), P()),
        out_specs=(split,) * 3,
        check_vma=False,
    )
```

time: 207 us -> 219 us (1.058)
  the two profiles are of different devices: /device:TPU:1 before, /device:TPU:38 now
where the time goes in v3:
time: 219 us; the launch traced here: 218 us
  Pallas kernels  208 us (95%)
  local copies, waits for them, and re-layouts  9.65 us (4%)
    pallas_call x1, Pallas kernels, bring(): pl.pallas_call(bring_kernel, name='bring', out_shape=(keys_shape, keys_sh...  93.9 us
    pallas_call x1, Pallas kernels, home(): pl.pallas_call(home_kernel, name='home', out_shape=(out_shape,) * 3, in_s...  81.8 us
    pallas_call x1, Pallas kernels, attend(): pl.pallas_call(attend_kernel, name='attend', out_shape=(query_shape, keys...  32.4 us
    unnamed x19, local copies, waits for them, and re-layouts  9.65 us

profile of v3, /device:TPU:38, one launch (start us, length us, event | category | flops | bytes accessed | tf_op | source)
XLA Modules:
  0.0 218.5 jit_solution(6524892317983875539)
XLA Ops:
  0.6 0.0 copy-start
  0.6 1.1 copy-done
  1.7 0.0 copy-start.1
  1.7 1.1 copy-done.1
  2.8 0.0 copy-start.2
  2.8 1.1 copy-done.2
  3.9 0.0 copy-start.3
  3.9 1.1 copy-done.3
  5.0 0.0 copy-start.5
  5.0 0.7 copy-done.5
  5.7 0.0 copy-start.6
  5.7 0.7 copy-done.6
  6.4 93.9 %bring.1 = (bf16[3,16,8,64,128]{4,3,2,1,0:T(8,128)(2,1)S(1)}, bf16[3,16,8,64,128]{4,3,2,1,0:T(8,128)(2,1)S(1)}, bf16[6,8,64,128]{3,2,1,0:T(8,128)(2,1)S(1)}, bf1...) custom-call(bf16[64,5120]{1,0:T(8,128)(2,1)S(1)} %copy-done, bf16[64,5120]{1,0:T(8,128)(2,1)S(1)} %copy-done.1, ...), custom_call_target="tpu_custom_call" | custom-call | tf_op jit(solution)/shard_map/bring/pallas_call | solution.py:355
  100.3 0.0 copy-start.4
  100.4 0.7 copy-done.4
  101.1 0.0 copy-start.7
  101.1 0.7 copy-done.7
  101.7 32.4 %attend.1 = (bf16[48,64,128]{2,1,0:T(8,128)(2,1)S(1)}, bf16[256,64,128]{2,1,0:T(8,128)(2,1)S(1)}, bf16[256,64,128]{2,1,0:T(8,128)(2,1)S(1)}) custom-call(s32[256]{0:T(256)S(1)} %copy-done.7, s32[16,256]{1,0:T(8,128)S(1)} %bitcast.19, bf16[48,64,128]{2,1,0:T(8,128)(2,1)S(1)} %bitcast.16, bf16[48,64,128]{2,1,0:T(8,128)(2,1)S(1)} %bitcast.17, ...), custom_call_target="tpu_custom_call" | custom-call | tf_op jit(solution)/shard_map/attend/pallas_call | solution.py:530
  134.1 81.8 %home.1 = (bf16[64,5120]{1,0:T(8,128)(2,1)S(1)}, bf16[64,5120]{1,0:T(8,128)(2,1)S(1)}, bf16[64,5120]{1,0:T(8,128)(2,1)S(1)}) custom-call(bf16[6,8,64,128]{3,2,1,0:T(8,128)(2,1)S(1)} %bitcast.15, bf16[32,8,64,128]{3,2,1,0:T(8,128)(2,1)S(1)} %bitcast.13, bf16[32,8,64,128]{3,2,1,0:T(8,128)(2,1)S(1)} %bitcast.14), custom_call_target="tpu_custom_call" | custom-call | tf_op jit(solution)/shard_map/home/pallas_call | solution.py:794
  216.0 0.8 copy.14
  216.8 0.8 copy.15
  217.7 0.8 copy.16
Async XLA Ops:
  0.6 1.1 copy-start
  1.7 1.1 copy-start.1
  2.8 1.1 copy-start.2
  3.9 1.1 copy-start.3
  5.0 0.7 copy-start.5
  5.7 0.7 copy-start.6
  100.3 0.7 copy-start.4
  101.1 0.7 copy-start.7

commit v4 on v2

--- a/solution.py
+++ b/solution.py
@@ -17,10 +17,10 @@
 PLANES = 8
 CHIPS = 16
 HEADS_PLANE = 5
-COPIES = 3
+COPIES = 2
 WORKERS = HEADS_PLANE * COPIES
 WIDTH = HEADS_PLANE * HDIM
-QGROUPS = 6
+QGROUPS = 8
 TOPK = 16
 SLOTS = 2 * CHIPS * PLANES
 UNITS = QGROUPS * PLANES
@@ -40,8 +40,14 @@
     return plane, chip, core
 
 
-def head_of(chip):
-    return jnp.minimum(chip // COPIES, HEADS_PLANE - 1)
+def role_of(chip):
+    x, y = chip % 4, chip // 4
+    even = y % 2 == 0
+    return even | (x == y - 1), jnp.where(even, x, HEADS_PLANE - 1), y // 2
+
+
+def chip_of(head, copy):
+    return jnp.where(head < HEADS_PLANE - 1, 8 * copy + head, 10 * copy + 4)
 
 
 def device_of(plane, chip, core):
@@ -131,7 +137,6 @@
 
     pack(0, k_in)
     start_stage(0)
-    start_stage(1)
     pack(1, v_in)
     pack(2, q_in)
 
@@ -154,48 +159,49 @@
         return 0
 
     lax.fori_loop(0, PLANES, gates, 0)
+    start_stage(1)
+    works, _, copy_here = role_of(chip)
 
     def share_keys(number, rows):
         landed, out = slabs[number], outs[number]
 
-        def step(d, _):
-            target = (chip + d) % CHIPS
-
-            @pl.when(target < WORKERS)
+        def step(m, _):
+            worker = (m + chip) % WORKERS
+            head = worker % HEADS_PLANE
+            target = chip_of(head, worker // HEADS_PLANE)
+            here, there = landed.at[head, :, rows], out.at[core * CHIPS + chip, :, rows]
+
+            @pl.when(target != chip)
             def _():
                 remote(
-                    landed.at[head_of(target), :, rows],
-                    out.at[core * CHIPS + chip, :, rows],
-                    psend.at[number], krecv.at[number, chip], device_of(plane, target, core),
+                    here, there, psend.at[number], krecv.at[number, chip],
+                    device_of(plane, target, core),
                 ).start()
 
-            return 0
-
-        lax.fori_loop(1, CHIPS, step, 0)
-
-        @pl.when(chip < WORKERS)
-        def _():
-            pltpu.make_async_copy(
-                landed.at[head_of(chip), :, rows],
-                out.at[core * CHIPS + chip, :, rows],
-                krecv.at[number, chip],
-            ).start()
+            @pl.when(target == chip)
+            def _():
+                pltpu.make_async_copy(here, there, krecv.at[number, chip]).start()
+
+            return 0
+
+        lax.fori_loop(0, WORKERS, step, 0)
 
     def share_queries(number, pick, place):
-        def step(j, _):
-            target = j * COPIES + chip % COPIES
+        def step(m, _):
+            j = (m + chip) % HEADS_PLANE
+            target = chip_of(j, copy_here)
 
             @pl.when(target != chip)
             def _():
                 remote(
-                    pick(j), place(chip // COPIES), psend.at[number],
+                    pick(j), place(chip % QGROUPS), psend.at[number],
                     qrecv.at[number - 2], device_of(plane, target, core),
                 ).start()
 
             @pl.when(target == chip)
             def _():
                 pltpu.make_async_copy(
-                    pick(j), place(chip // COPIES), qrecv.at[number - 2]
+                    pick(j), place(chip % QGROUPS), qrecv.at[number - 2]
                 ).start()
 
             return 0
@@ -222,7 +228,7 @@
 
     sibling = device_of(plane, chip, 1 - core)
 
-    @pl.when(chip < WORKERS)
+    @pl.when(works)
     def _():
         for number, out in ((0, kh), (1, vh)):
             def forward(d, _, number=number, out=out):
@@ -234,15 +240,8 @@
 
             lax.fori_loop(0, CHIPS, forward, 0)
 
-        @pl.when(chip % COPIES == 0)
-        def _():
-            for number, out in enumerate((qh, fh, ph)):
-                take_bytes(out, qrecv.at[number])
-
-        @pl.when(chip % COPIES != 0)
-        def _():
-            for number, out in enumerate((qh, fh, ph)):
-                take_bytes(out.at[pl.ds(0, QGROUPS - 1)], qrecv.at[number])
+        for number, out in enumerate((qh, fh, ph)):
+            take_bytes(out, qrecv.at[number])
 
         for number, out in ((0, kh), (1, vh)):
             theirs = out.at[pl.ds((1 - core) * CHIPS, CHIPS)]
@@ -254,19 +253,19 @@
         take_bytes(landed, zsend.at[stage])
     take_bytes(pz.at[pl.ds(0, PLANES - 1)], zsend.at[STAGES])
 
-    @pl.when(chip < WORKERS)
+    def drain(keys, queries):
+        for number, out in ((0, kh), (1, vh)):
+            take_bytes(out.at[pl.ds(0, keys)], psend.at[number])
+        for number, out in ((2, qh), (3, fh), (4, ph)):
+            take_bytes(out.at[pl.ds(0, queries)], psend.at[number])
+
+    @pl.when(works)
     def _():
-        for number, out in ((0, kh), (1, vh)):
-            take_bytes(out.at[pl.ds(0, WORKERS - 1)], psend.at[number])
-        for number, out in ((2, qh), (3, fh), (4, ph)):
-            take_bytes(out.at[pl.ds(0, HEADS_PLANE - 1)], psend.at[number])
-
-    @pl.when(chip >= WORKERS)
+        drain(WORKERS - 1, HEADS_PLANE - 1)
+
+    @pl.when(jnp.logical_not(works))
     def _():
-        for number, out in ((0, kh), (1, vh)):
-            take_bytes(out.at[pl.ds(0, WORKERS)], psend.at[number])
-        for number, out in ((2, qh), (3, fh), (4, ph)):
-            take_bytes(out.at[pl.ds(0, HEADS_PLANE)], psend.at[number])
+        drain(WORKERS, HEADS_PLANE)
 
 
 def bring(keys_in, values, queries, grad_out, fine_gate, coarse_gate):
@@ -315,53 +314,58 @@
 def attend_kernel(
     toc, sel, q, fg, pg, k, v,
     dq, dk, dv,
-    ak, av, pk, pv, pq, cdq, part, cot, soc,
+    acc, wide, pk, pv, pq, cdq, part_k, part_v, cot, soc,
 ):
     _, chip, core = where_am_i()
-    head, replica = chip // COPIES, chip % COPIES
-    groups = jnp.where(replica == 0, QGROUPS, QGROUPS - 1)
-    groups = jnp.where(chip < WORKERS, groups, 0)
-    units = groups * PLANES
+    works, head, copy = role_of(chip)
+    units = jnp.where(works, UNITS, 0)
     factor = 1.0 / math.sqrt(HDIM)
     log2e = math.log2(math.e)
 
-    def invert(cube, _):
-        tile = toc[cube]
-        cot[tile] = cube
-        soc[cube] = (
-            lax.shift_left(lax.shift_right_logical(tile, 3) & 1, 7)
-            + lax.shift_left(lax.shift_right_logical(tile, 4) & 1, 6)
-            + lax.shift_left(tile & 7, 3)
-            + lax.shift_right_logical(tile, 5)
-        )
+    def eighths(source, group):
+        block = source[pl.ds(pl.multiple_of(group * 8, 8), 8)].astype(F32)
+        return jnp.sum(block.reshape(8, 8, 8, HDIM), axis=1).reshape(64, HDIM)
+
+    def prepare(group, _):
+        rows = pl.ds(pl.multiple_of(group * 64, 64), 64)
+        part_k[rows, :] = eighths(k, group)
+        part_v[rows, :] = eighths(v, group)
+        acc[pl.ds(pl.multiple_of(group * 8, 8), 8)] = jnp.zeros((8, CUBE, 2 * HDIM), F32)
+        for i in range(8):
+            cube = group * 8 + i
+            tile = toc[cube]
+            cot[tile] = cube
+            soc[cube] = (
+                lax.shift_left(lax.shift_right_logical(tile, 3) & 1, 7)
+                + lax.shift_left(lax.shift_right_logical(tile, 4) & 1, 6)
+                + lax.shift_left(tile & 7, 3)
+                + lax.shift_right_logical(tile, 5)
+            )
         return 0
 
-    lax.fori_loop(0, SLOTS, invert, 0, unroll=8)
-
-    def pool(source, groups, into):
-        def gather(group, _):
-            block = source[pl.ds(pl.multiple_of(group * 8, 8), 8)].astype(F32)
-            halves = jnp.sum(block.reshape(8, 8, 8, HDIM), axis=1)
-            part[pl.ds(pl.multiple_of(group * 64, 64), 64), :] = halves.reshape(64, HDIM)
-            return 0
-
-        lax.fori_loop(0, groups, gather, 0, unroll=2)
+    lax.fori_loop(0, SLOTS // 8, prepare, 0)
+
+    def pool(part, into):
         count = into.shape[0]
         total = part[pl.ds(0, count, stride=8), :]
         for row in range(1, 8):
             total += part[pl.ds(row, count, stride=8), :]
         into[...] = total * (1.0 / CUBE)
 
-    pool(k, SLOTS // 8, pk)
-    pool(v, SLOTS // 8, pv)
-    pool(q, UNITS // 8, pq)
-    unit_at = lax.broadcasted_iota(jnp.int32, (UNITS, 16, HDIM), 0)
+    pool(part_k, pk)
+    pool(part_v, pv)
+
+    def prepare_queries(group, _):
+        part_k[pl.ds(pl.multiple_of(group * 64, 64), 64), :] = eighths(q, group)
+        return 0
+
+    lax.fori_loop(0, QGROUPS, prepare_queries, 0)
+    pool(part_k, pq)
     row_at = lax.broadcasted_iota(jnp.int32, (UNITS, 16, HDIM), 1)
     pooled_g = jnp.sum(
-        jnp.where((unit_at < units) & (row_at == head), pg[...].astype(F32), 0.0), axis=1
+        jnp.where(row_at == head, pg[...].astype(F32), 0.0), axis=1
     ).astype(BF16)
-    live = lax.broadcasted_iota(jnp.int32, (UNITS, HDIM), 0) < units
-    pooled_q = jnp.where(live, pq[...], 0.0).astype(BF16)
+    pooled_q = pq[...].astype(BF16)
     pooled_k = pk[...].astype(BF16)
     pooled_v = pv[...].astype(BF16)
     scores = nt(pooled_q, pooled_k) * factor
@@ -371,19 +375,12 @@
     inner = jnp.sum(probs * dprobs, axis=1, keepdims=True)
     dscores = (probs * (dprobs - inner)).astype(BF16)
     cdq[...] = nn(dscores, pooled_k) * (factor / CUBE)
-    pk[...] = tn(dscores, pooled_q) * (1.0 / CUBE)
+    pk[...] = tn(dscores, pooled_q) * (factor / CUBE)
     pv[...] = tn(probs.astype(BF16), pooled_g) * (1.0 / CUBE)
-
-    def fill(slot, _):
-        ak[slot] = jnp.broadcast_to(pk[pl.ds(slot, 1), :], (CUBE, HDIM))
-        av[slot] = jnp.broadcast_to(pv[pl.ds(slot, 1), :], (CUBE, HDIM))
-        return 0
-
-    lax.fori_loop(0, SLOTS, fill, 0, unroll=4)
+    wide[...] = jnp.zeros_like(wide)
 
     def listed(n):
-        origin = n // PLANES * COPIES + replica
-        tile = ((n % PLANES * 4) + origin // 8 * 2 + core) * 8 + origin % 8
+        tile = (n % PLANES * 4 + copy * 2 + core) * 8 + n // PLANES
         cube = cot[tile]
         slots = [soc[sel[r, cube]] for r in range(TOPK)]
         return [slots[c * 4:c * 4 + 4] for c in range(4)]
@@ -391,46 +388,45 @@
     def tiles_of(ref, quarter):
         return jnp.concatenate([ref[s] for s in quarter], axis=0)
 
-    def softmax_terms(n, quarters):
-        score = [nt(q[n], tiles_of(k, quarter)) for quarter in quarters]
-        dprob = [nt(fg[n], tiles_of(v, quarter)) for quarter in quarters]
-        top = functools.reduce(jnp.maximum, score)
-        top = jnp.max(top, axis=1, keepdims=True)
+    def pair(m, _):
+        numbers = (2 * m, 2 * m + 1)
+        lists = [listed(n) for n in numbers]
+        for i, n in enumerate(numbers):
+            wide[0, i * CUBE:(i + 1) * CUBE, i * HDIM:(i + 1) * HDIM] = q[n]
+            wide[1, i * CUBE:(i + 1) * CUBE, i * HDIM:(i + 1) * HDIM] = fg[n]
+        beside = lambda ref, c: jnp.concatenate([tiles_of(ref, quarters[c]) for quarters in lists], axis=1)
+        score = [nt(beside(k, c), wide[0]) for c in range(4)]
+        dprob = [nt(beside(v, c), wide[1]) for c in range(4)]
+        top = jnp.max(functools.reduce(jnp.maximum, score), axis=0, keepdims=True)
         weight = [jnp.exp2((s - top) * (factor * log2e)) for s in score]
-        total = jnp.sum(functools.reduce(jnp.add, weight), axis=1, keepdims=True)
+        total = jnp.sum(functools.reduce(jnp.add, weight), axis=0, keepdims=True)
         inverse = 1.0 / total
         mixed = functools.reduce(jnp.add, [w * d for w, d in zip(weight, dprob)])
-        center = jnp.sum(mixed, axis=1, keepdims=True) * inverse
-        probs = [w * inverse for w in weight]
-        dscore = [(p * (d - center)).astype(BF16) for p, d in zip(probs, dprob)]
-        return [p.astype(BF16) for p in probs], dscore
-
-    def spread_terms(n, quarters, probs, dscore):
-        query, grad = q[n], fg[n]
-        dquery = jnp.zeros((CUBE, HDIM), F32)
-        for c, quarter in enumerate(quarters):
-            dquery += nn(dscore[c], tiles_of(k, quarter))
-            key_terms = tn(dscore[c], query)
-            value_terms = tn(probs[c], grad)
-            for i, s in enumerate(quarter):
-                ak[s] += key_terms[i * CUBE:(i + 1) * CUBE]
-                av[s] += value_terms[i * CUBE:(i + 1) * CUBE]
-        dq[n] = (dquery * factor + cdq[pl.ds(n, 1), :]).astype(BF16)
-
-    def pair(m, _):
-        numbers = [2 * m, 2 * m + 1]
-        lists = [listed(n) for n in numbers]
-        terms = [softmax_terms(n, quarters) for n, quarters in zip(numbers, lists)]
-        for n, quarters, (probs, dscore) in zip(numbers, lists, terms):
-            spread_terms(n, quarters, probs, dscore)
+        center = jnp.sum(mixed, axis=0, keepdims=True) * inverse
+        dquery = jnp.zeros((2 * CUBE, 2 * HDIM), F32)
+        for c in range(4):
+            prob = weight[c] * inverse
+            dscore = (prob * (dprob[c] - center)).astype(BF16)
+            dquery += tn(dscore, beside(k, c))
+            key_terms = nn(dscore, wide[0])
+            value_terms = nn(prob.astype(BF16), wide[1])
+            for i, quarters in enumerate(lists):
+                for at, s in enumerate(quarters[c]):
+                    rows, lanes = slice(at * CUBE, (at + 1) * CUBE), slice(i * HDIM, (i + 1) * HDIM)
+                    acc[s, :, :HDIM] += key_terms[rows, lanes]
+                    acc[s, :, HDIM:] += value_terms[rows, lanes]
+        for i, n in enumerate(numbers):
+            mine = dquery[i * CUBE:(i + 1) * CUBE, i * HDIM:(i + 1) * HDIM]
+            dq[n] = (mine * factor + cdq[pl.ds(n, 1), :]).astype(BF16)
         return 0
 
     lax.fori_loop(0, units // 2, pair, 0)
 
     def finish(group, _):
-        rows = pl.ds(pl.multiple_of(group * 4, 4), 4)
-        dk[rows] = (ak[rows] * factor).astype(BF16)
-        dv[rows] = av[rows].astype(BF16)
+        for i in range(4):
+            slot = group * 4 + i
+            dk[slot] = (acc[slot, :, :HDIM] * factor + pk[pl.ds(slot, 1), :]).astype(BF16)
+            dv[slot] = (acc[slot, :, HDIM:] + pv[pl.ds(slot, 1), :]).astype(BF16)
         return 0
 
     lax.fori_loop(0, SLOTS // 4, finish, 0)
@@ -448,12 +444,13 @@
         in_specs=[smem] * 2 + [vmem] * 5,
         out_specs=[vmem] * 3,
         scratch_shapes=[
-            pltpu.VMEM((SLOTS, CUBE, HDIM), F32),
-            pltpu.VMEM((SLOTS, CUBE, HDIM), F32),
+            pltpu.VMEM((SLOTS, CUBE, 2 * HDIM), F32),
+            pltpu.VMEM((2, 2 * CUBE, 2 * HDIM), BF16),
             pltpu.VMEM((SLOTS, HDIM), F32),
             pltpu.VMEM((SLOTS, HDIM), F32),
             pltpu.VMEM((UNITS, HDIM), F32),
             pltpu.VMEM((UNITS, HDIM), F32),
+            pltpu.VMEM((SLOTS * 8, HDIM), F32),
             pltpu.VMEM((SLOTS * 8, HDIM), F32),
             pltpu.SMEM((SLOTS,), jnp.int32),
             pltpu.SMEM((SLOTS,), jnp.int32),
@@ -473,8 +470,7 @@
     ssend, srecv, psend, precv, zsend, zrecv,
 ):
     plane, chip, core = where_am_i()
-    head, replica = head_of(chip), chip % COPIES
-    works = chip < WORKERS
+    works, head, replica = role_of(chip)
     greet(plane, chip, core)
     sibling = device_of(plane, chip, 1 - core)
     sources, owns, sibs = (dk, dv), (own_k, own_v), (sib_k, sib_v)
@@ -494,18 +490,18 @@
 
             lax.fori_loop(0, CHIPS, give, 0)
 
-        def send_query(i, _):
-            wanted = i * COPIES + replica
-            target = jnp.minimum(wanted, CHIPS - 1)
-
-            @pl.when((wanted < CHIPS) & (target != chip))
+        def send_query(m, _):
+            i = (m + chip) % QGROUPS
+            target = replica * QGROUPS + i
+
+            @pl.when(target != chip)
             def _():
                 remote(
                     dq.at[i], land_q.at[head], psend.at[2], precv.at[4],
                     device_of(plane, target, core),
                 ).start()
 
-            @pl.when(wanted == chip)
+            @pl.when(target == chip)
             def _():
                 pltpu.make_async_copy(dq.at[i], land_q.at[head], precv.at[4]).start()
 
@@ -606,13 +602,7 @@
             take_bytes(sibs[number], ssend.at[number])
             take_bytes(owns[number].at[pl.ds(0, CHIPS - 1)], psend.at[number])
 
-        @pl.when(replica == 0)
-        def _():
-            take_bytes(dq.at[pl.ds(0, QGROUPS - 1)], psend.at[2])
-
-        @pl.when(replica != 0)
-        def _():
-            take_bytes(dq.at[pl.ds(0, QGROUPS - 2)], psend.at[2])
+        take_bytes(dq.at[pl.ds(0, QGROUPS - 1)], psend.at[2])
 
 
 def home(dq, dk, dv, rows, width):

time: 207 us -> 215 us (1.039)
  Pallas kernels: 195 us -> 204 us
    pallas_call x1, Pallas kernels: 84.2 us -> 90.9 us  [bring(): pl.pallas_call(bring_kernel, name='bring', out_shape=(keys_shape, keys_sh...]
    pallas_call x1, Pallas kernels: 34.4 us -> 39.6 us  [attend(): pl.pallas_call(attend_kernel, name='attend', out_shape=(query_shape, keys...]
    pallas_call x1, Pallas kernels: 75.9 us -> 73.7 us  [home(): pl.pallas_call(home_kernel, name='home', out_shape=(out_shape,) * 3, in_s...]
where the time goes in v4:
time: 215 us; the launch traced here: 214 us
  Pallas kernels  204 us (95%)
  local copies, waits for them, and re-layouts  9.65 us (4%)
    pallas_call x1, Pallas kernels, bring(): pl.pallas_call(bring_kernel, name='bring', out_shape=(keys_shape, keys_sh...  90.9 us
    pallas_call x1, Pallas kernels, home(): pl.pallas_call(home_kernel, name='home', out_shape=(out_shape,) * 3, in_s...  73.7 us
    pallas_call x1, Pallas kernels, attend(): pl.pallas_call(attend_kernel, name='attend', out_shape=(query_shape, keys...  39.6 us
    unnamed x19, local copies, waits for them, and re-layouts  9.65 us

profile of v4, /device:TPU:1, one launch (start us, length us, event | category | flops | bytes accessed | tf_op | source)
XLA Modules:
  0.0 214.5 jit_solution(14355830338642237136)
XLA Ops:
  0.6 0.0 copy-start
  0.6 1.1 copy-done
  1.7 0.0 copy-start.1
  1.7 1.1 copy-done.1
  2.8 0.0 copy-start.2
  2.8 1.1 copy-done.2
  3.9 0.0 copy-start.3
  3.9 1.1 copy-done.3
  5.0 0.0 copy-start.5
  5.0 0.7 copy-done.5
  5.7 0.0 copy-start.6
  5.7 0.7 copy-done.6
  6.4 90.9 %bring.1 = (bf16[32,8,64,128]{3,2,1,0:T(8,128)(2,1)S(1)}, bf16[32,8,64,128]{3,2,1,0:T(8,128)(2,1)S(1)}, bf16[8,8,64,128]{3,2,1,0:T(8,128)(2,1)S(1)}, bf16[8,8,64...) custom-call(bf16[64,5120]{1,0:T(8,128)(2,1)S(1)} %copy-done, bf16[64,5120]{1,0:T(8,128)(2,1)S(1)} %copy-done.1, ...), custom_call_target="tpu_custom_call" | custom-call | tf_op jit(solution)/shard_map/bring/pallas_call | solution.py:279
  97.3 0.0 copy-start.4
  97.3 0.7 copy-done.4
  98.0 0.0 copy-start.7
  98.0 0.7 copy-done.7
  98.7 39.6 %attend.1 = (bf16[64,64,128]{2,1,0:T(8,128)(2,1)S(1)}, bf16[256,64,128]{2,1,0:T(8,128)(2,1)S(1)}, bf16[256,64,128]{2,1,0:T(8,128)(2,1)S(1)}) custom-call(s32[256]{0:T(256)S(1)} %copy-done.7, s32[16,256]{1,0:T(8,128)S(1)} %bitcast.19, bf16[64,64,128]{2,1,0:T(8,128)(2,1)S(1)} %bitcast.16, bf16[64,64,128]{2,1,0:T(8,128)(2,1)S(1)} %bitcast.17, ...), custom_call_target="tpu_custom_call" | custom-call | tf_op jit(solution)/shard_map/attend/pallas_call | solution.py:440
  138.3 73.7 %home.1 = (bf16[64,5120]{1,0:T(8,128)(2,1)S(1)}, bf16[64,5120]{1,0:T(8,128)(2,1)S(1)}, bf16[64,5120]{1,0:T(8,128)(2,1)S(1)}) custom-call(bf16[8,8,64,128]{3,2,1,0:T(8,128)(2,1)S(1)} %bitcast.15, bf16[32,8,64,128]{3,2,1,0:T(8,128)(2,1)S(1)} %bitcast.11, bf16[32,8,64,128]{3,2,1,0:T(8,128)(2,1)S(1)} %bitcast.12), custom_call_target="tpu_custom_call" | custom-call | tf_op jit(solution)/shard_map/home/pallas_call | solution.py:616
  212.0 0.8 copy.14
  212.8 0.8 copy.15
  213.6 0.8 copy.16
Async XLA Ops:
  0.6 1.1 copy-start
  1.7 1.1 copy-start.1
  2.8 1.1 copy-start.2
  3.9 1.1 copy-start.3
  5.0 0.7 copy-start.5
  5.7 0.7 copy-start.6
  97.3 0.7 copy-start.4
  98.0 0.7 copy-start.7

commit v5 on v4

--- a/solution.py
+++ b/solution.py
@@ -42,12 +42,25 @@
 
 def role_of(chip):
     x, y = chip % 4, chip // 4
-    even = y % 2 == 0
-    return even | (x == y - 1), jnp.where(even, x, HEADS_PLANE - 1), y // 2
+    plain = y % 2 == x % 2
+    return plain | ((y % 2 == 1) & (x == y - 1)), jnp.where(plain, x, HEADS_PLANE - 1), y // 2
 
 
 def chip_of(head, copy):
-    return jnp.where(head < HEADS_PLANE - 1, 8 * copy + head, 10 * copy + 4)
+    return jnp.where(head < HEADS_PLANE - 1, head % 2 * 4 + 8 * copy + head, 10 * copy + 4)
+
+
+def lean_of(head):
+    return jnp.where(head < HEADS_PLANE - 1, 0, 3)
+
+
+def asks(head, chip):
+    turned = (chip // 4 + lean_of(head)) % 4
+    return turned // 2, turned % 2 * 4 + chip % 4
+
+
+def asked_by(head, copy, group):
+    return (2 * copy + group // 4 + 4 - lean_of(head)) % 4 * 4 + group % 4
 
 
 def device_of(plane, chip, core):
@@ -160,7 +173,7 @@
 
     lax.fori_loop(0, PLANES, gates, 0)
     start_stage(1)
-    works, _, copy_here = role_of(chip)
+    works, _, _ = role_of(chip)
 
     def share_keys(number, rows):
         landed, out = slabs[number], outs[number]
@@ -189,19 +202,20 @@
     def share_queries(number, pick, place):
         def step(m, _):
             j = (m + chip) % HEADS_PLANE
-            target = chip_of(j, copy_here)
+            copy, group = asks(j, chip)
+            target = chip_of(j, copy)
 
             @pl.when(target != chip)
             def _():
                 remote(
-                    pick(j), place(chip % QGROUPS), psend.at[number],
+                    pick(j), place(group), psend.at[number],
                     qrecv.at[number - 2], device_of(plane, target, core),
                 ).start()
 
             @pl.when(target == chip)
             def _():
                 pltpu.make_async_copy(
-                    pick(j), place(chip % QGROUPS), qrecv.at[number - 2]
+                    pick(j), place(group), qrecv.at[number - 2]
                 ).start()
 
             return 0
@@ -314,7 +328,8 @@
 def attend_kernel(
     toc, sel, q, fg, pg, k, v,
     dq, dk, dv,
-    acc, wide, pk, pv, pq, cdq, part_k, part_v, cot, soc,
+    ak, av, wide_0, wide_1, prob_0, prob_1, dsc_0, dsc_1,
+    pk, pv, pq, cdq, part_k, part_v, cot, soc, held,
 ):
     _, chip, core = where_am_i()
     works, head, copy = role_of(chip)
@@ -330,7 +345,8 @@
         rows = pl.ds(pl.multiple_of(group * 64, 64), 64)
         part_k[rows, :] = eighths(k, group)
         part_v[rows, :] = eighths(v, group)
-        acc[pl.ds(pl.multiple_of(group * 8, 8), 8)] = jnp.zeros((8, CUBE, 2 * HDIM), F32)
+        for total_of in (ak, av):
+            total_of[pl.ds(pl.multiple_of(group * 8, 8), 8)] = jnp.zeros((8, CUBE, HDIM), F32)
         for i in range(8):
             cube = group * 8 + i
             tile = toc[cube]
@@ -377,56 +393,84 @@
     cdq[...] = nn(dscores, pooled_k) * (factor / CUBE)
     pk[...] = tn(dscores, pooled_q) * (factor / CUBE)
     pv[...] = tn(probs.astype(BF16), pooled_g) * (1.0 / CUBE)
-    wide[...] = jnp.zeros_like(wide)
+    wide_0[...] = jnp.zeros_like(wide_0)
+    wide_1[...] = jnp.zeros_like(wide_1)
 
     def listed(n):
-        tile = (n % PLANES * 4 + copy * 2 + core) * 8 + n // PLANES
+        origin = asked_by(head, copy, n // PLANES)
+        tile = (n % PLANES * 4 + origin // 8 * 2 + core) * 8 + origin % 8
         cube = cot[tile]
-        slots = [soc[sel[r, cube]] for r in range(TOPK)]
-        return [slots[c * 4:c * 4 + 4] for c in range(4)]
-
-    def tiles_of(ref, quarter):
-        return jnp.concatenate([ref[s] for s in quarter], axis=0)
-
-    def pair(m, _):
-        numbers = (2 * m, 2 * m + 1)
-        lists = [listed(n) for n in numbers]
-        for i, n in enumerate(numbers):
-            wide[0, i * CUBE:(i + 1) * CUBE, i * HDIM:(i + 1) * HDIM] = q[n]
-            wide[1, i * CUBE:(i + 1) * CUBE, i * HDIM:(i + 1) * HDIM] = fg[n]
-        beside = lambda ref, c: jnp.concatenate([tiles_of(ref, quarters[c]) for quarters in lists], axis=1)
-        score = [nt(beside(k, c), wide[0]) for c in range(4)]
-        dprob = [nt(beside(v, c), wide[1]) for c in range(4)]
+        return [soc[sel[r, cube]] for r in range(TOPK)]
+
+    def beside(ref, lists, c):
+        return jnp.concatenate(
+            [jnp.concatenate([ref[s] for s in slots[c * 4:c * 4 + 4]], axis=0) for slots in lists],
+            axis=1,
+        )
+
+    sides = ((prob_0, dsc_0, wide_0), (prob_1, dsc_1, wide_1))
+
+    def advance(old, m_old, new, m_new):
+        prob_new, dsc_new, wide_new = sides[new]
+        lists_new = [listed(2 * m_new + i) for i in range(2)]
+        for i, slots in enumerate(lists_new):
+            for r, slot in enumerate(slots):
+                held[new, i * TOPK + r] = slot
+            rows, lanes = slice(i * CUBE, (i + 1) * CUBE), slice(i * HDIM, (i + 1) * HDIM)
+            wide_new[0, rows, lanes] = q[2 * m_new + i]
+            wide_new[1, rows, lanes] = fg[2 * m_new + i]
+        score, dprob = [], []
+        if old is not None:
+            prob_old, dsc_old, wide_old = sides[old]
+            lists_old = [[held[old, i * TOPK + r] for r in range(TOPK)] for i in range(2)]
+            dquery = jnp.zeros((2 * CUBE, 2 * HDIM), F32)
+        for c in range(4):
+            score.append(nt(beside(k, lists_new, c), wide_new[0]))
+            dprob.append(nt(beside(v, lists_new, c), wide_new[1]))
+            if old is None:
+                continue
+            chunk = slice(c * 4 * CUBE, (c + 1) * 4 * CUBE)
+            dscore = dsc_old[chunk]
+            dquery += tn(dscore, beside(k, lists_old, c))
+            key_terms = nn(dscore, wide_old[0])
+            value_terms = nn(prob_old[chunk], wide_old[1])
+            for i, slots in enumerate(lists_old):
+                lanes = slice(i * HDIM, (i + 1) * HDIM)
+                for total_of, terms in ((ak, key_terms), (av, value_terms)):
+                    before = [total_of[s] for s in slots[c * 4:c * 4 + 4]]
+                    for at, s in enumerate(slots[c * 4:c * 4 + 4]):
+                        total_of[s] = before[at] + terms[at * CUBE:(at + 1) * CUBE, lanes]
         top = jnp.max(functools.reduce(jnp.maximum, score), axis=0, keepdims=True)
         weight = [jnp.exp2((s - top) * (factor * log2e)) for s in score]
         total = jnp.sum(functools.reduce(jnp.add, weight), axis=0, keepdims=True)
         inverse = 1.0 / total
         mixed = functools.reduce(jnp.add, [w * d for w, d in zip(weight, dprob)])
         center = jnp.sum(mixed, axis=0, keepdims=True) * inverse
-        dquery = jnp.zeros((2 * CUBE, 2 * HDIM), F32)
         for c in range(4):
+            chunk = slice(c * 4 * CUBE, (c + 1) * 4 * CUBE)
             prob = weight[c] * inverse
-            dscore = (prob * (dprob[c] - center)).astype(BF16)
-            dquery += tn(dscore, beside(k, c))
-            key_terms = nn(dscore, wide[0])
-            value_terms = nn(prob.astype(BF16), wide[1])
-            for i, quarters in enumerate(lists):
-                for at, s in enumerate(quarters[c]):
-                    rows, lanes = slice(at * CUBE, (at + 1) * CUBE), slice(i * HDIM, (i + 1) * HDIM)
-                    acc[s, :, :HDIM] += key_terms[rows, lanes]
-                    acc[s, :, HDIM:] += value_terms[rows, lanes]
-        for i, n in enumerate(numbers):
-            mine = dquery[i * CUBE:(i + 1) * CUBE, i * HDIM:(i + 1) * HDIM]
-            dq[n] = (mine * factor + cdq[pl.ds(n, 1), :]).astype(BF16)
+            prob_new[chunk] = prob.astype(BF16)
+            dsc_new[chunk] = (prob * (dprob[c] - center)).astype(BF16)
+        if old is not None:
+            for i in range(2):
+                n = 2 * m_old + i
+                mine = dquery[i * CUBE:(i + 1) * CUBE, i * HDIM:(i + 1) * HDIM]
+                dq[n] = (mine * factor + cdq[pl.ds(n, 1), :]).astype(BF16)
+
+    advance(None, 0, 0, 0)
+
+    def two_pairs(m, _):
+        advance(0, 2 * m, 1, 2 * m + 1)
+        advance(1, 2 * m + 1, 0, jnp.minimum(2 * m + 2, UNITS // 2 - 1))
         return 0
 
-    lax.fori_loop(0, units // 2, pair, 0)
+    lax.fori_loop(0, units // 4, two_pairs, 0)
 
     def finish(group, _):
         for i in range(4):
             slot = group * 4 + i
-            dk[slot] = (acc[slot, :, :HDIM] * factor + pk[pl.ds(slot, 1), :]).astype(BF16)
-            dv[slot] = (acc[slot, :, HDIM:] + pv[pl.ds(slot, 1), :]).astype(BF16)
+            dk[slot] = (ak[slot] * factor + pk[pl.ds(slot, 1), :]).astype(BF16)
+            dv[slot] = (av[slot] + pv[pl.ds(slot, 1), :]).astype(BF16)
         return 0
 
     lax.fori_loop(0, SLOTS // 4, finish, 0)
@@ -444,8 +488,14 @@
         in_specs=[smem] * 2 + [vmem] * 5,
         out_specs=[vmem] * 3,
         scratch_shapes=[
-            pltpu.VMEM((SLOTS, CUBE, 2 * HDIM), F32),
+            pltpu.VMEM((SLOTS, CUBE, HDIM), F32),
+            pltpu.VMEM((SLOTS, CUBE, HDIM), F32),
             pltpu.VMEM((2, 2 * CUBE, 2 * HDIM), BF16),
+            pltpu.VMEM((2, 2 * CUBE, 2 * HDIM), BF16),
+            pltpu.VMEM((TOPK * CUBE, 2 * CUBE), BF16),
+            pltpu.VMEM((TOPK * CUBE, 2 * CUBE), BF16),
+            pltpu.VMEM((TOPK * CUBE, 2 * CUBE), BF16),
+            pltpu.VMEM((TOPK * CUBE, 2 * CUBE), BF16),
             pltpu.VMEM((SLOTS, HDIM), F32),
             pltpu.VMEM((SLOTS, HDIM), F32),
             pltpu.VMEM((UNITS, HDIM), F32),
@@ -454,6 +504,7 @@
             pltpu.VMEM((SLOTS * 8, HDIM), F32),
             pltpu.SMEM((SLOTS,), jnp.int32),
             pltpu.SMEM((SLOTS,), jnp.int32),
+            pltpu.SMEM((2, 2 * TOPK), jnp.int32),
         ],
         compiler_params=pltpu.CompilerParams(vmem_limit_bytes=ATTEND_VMEM),
     )(
@@ -492,7 +543,7 @@
 
         def send_query(m, _):
             i = (m + chip) % QGROUPS
-            target = replica * QGROUPS + i
+            target = asked_by(head, replica, i)
 
             @pl.when(target != chip)
             def _():

time: 215 us -> 211 us (0.981)
  Pallas kernels: 204 us -> 199 us
    pallas_call x1, Pallas kernels: 90.9 us -> 80.8 us  [bring(): pl.pallas_call(bring_kernel, name='bring', out_shape=(keys_shape, keys_sh...]
    pallas_call x1, Pallas kernels: 73.7 us -> 80.9 us  [home(): pl.pallas_call(home_kernel, name='home', out_shape=(out_shape,) * 3, in_s...]
where the time goes in v5:
time: 211 us; the launch traced here: 210 us
  Pallas kernels  199 us (94%)
  local copies, waits for them, and re-layouts  9.65 us (5%)
    pallas_call x1, Pallas kernels, home(): pl.pallas_call(home_kernel, name='home', out_shape=(out_shape,) * 3, in_s...  80.9 us
    pallas_call x1, Pallas kernels, bring(): pl.pallas_call(bring_kernel, name='bring', out_shape=(keys_shape, keys_sh...  80.8 us
    pallas_call x1, Pallas kernels, attend(): pl.pallas_call(attend_kernel, name='attend', out_shape=(query_shape, keys...  37.6 us
    unnamed x19, local copies, waits for them, and re-layouts  9.65 us

profile of v5, /device:TPU:1, one launch (start us, length us, event | category | flops | bytes accessed | tf_op | source)
XLA Modules:
  0.0 209.6 jit_solution(16486812002597941064)
XLA Ops:
  0.6 0.0 copy-start
  0.6 1.1 copy-done
  1.7 0.0 copy-start.1
  1.7 1.1 copy-done.1
  2.8 0.0 copy-start.2
  2.8 1.1 copy-done.2
  3.9 0.0 copy-start.3
  3.9 1.1 copy-done.3
  5.0 0.0 copy-start.5
  5.0 0.7 copy-done.5
  5.7 0.0 copy-start.6
  5.7 0.7 copy-done.6
  6.4 80.8 %bring.1 = (bf16[32,8,64,128]{3,2,1,0:T(8,128)(2,1)S(1)}, bf16[32,8,64,128]{3,2,1,0:T(8,128)(2,1)S(1)}, bf16[8,8,64,128]{3,2,1,0:T(8,128)(2,1)S(1)}, bf16[8,8,64...) custom-call(bf16[64,5120]{1,0:T(8,128)(2,1)S(1)} %copy-done, bf16[64,5120]{1,0:T(8,128)(2,1)S(1)} %copy-done.1, ...), custom_call_target="tpu_custom_call" | custom-call | tf_op jit(solution)/shard_map/bring/pallas_call | solution.py:293
  87.2 0.0 copy-start.4
  87.2 0.7 copy-done.4
  87.9 0.0 copy-start.7
  87.9 0.7 copy-done.7
  88.6 37.6 %attend.1 = (bf16[64,64,128]{2,1,0:T(8,128)(2,1)S(1)}, bf16[256,64,128]{2,1,0:T(8,128)(2,1)S(1)}, bf16[256,64,128]{2,1,0:T(8,128)(2,1)S(1)}) custom-call(s32[256]{0:T(256)S(1)} %copy-done.7, s32[16,256]{1,0:T(8,128)S(1)} %bitcast.19, bf16[64,64,128]{2,1,0:T(8,128)(2,1)S(1)} %bitcast.16, bf16[64,64,128]{2,1,0:T(8,128)(2,1)S(1)} %bitcast.17, ...), custom_call_target="tpu_custom_call" | custom-call | tf_op jit(solution)/shard_map/attend/pallas_call | solution.py:484
  126.2 80.9 %home.1 = (bf16[64,5120]{1,0:T(8,128)(2,1)S(1)}, bf16[64,5120]{1,0:T(8,128)(2,1)S(1)}, bf16[64,5120]{1,0:T(8,128)(2,1)S(1)}) custom-call(bf16[8,8,64,128]{3,2,1,0:T(8,128)(2,1)S(1)} %bitcast.15, bf16[32,8,64,128]{3,2,1,0:T(8,128)(2,1)S(1)} %bitcast.11, bf16[32,8,64,128]{3,2,1,0:T(8,128)(2,1)S(1)} %bitcast.12), custom_call_target="tpu_custom_call" | custom-call | tf_op jit(solution)/shard_map/home/pallas_call | solution.py:667
  207.1 0.8 copy.14
  207.9 0.8 copy.15
  208.8 0.8 copy.16
Async XLA Ops:
  0.6 1.1 copy-start
  1.7 1.1 copy-start.1
  2.8 1.1 copy-start.2
  3.9 1.1 copy-start.3
  5.0 0.7 copy-start.5
  5.7 0.7 copy-start.6
  87.2 0.7 copy-start.4
  87.9 0.7 copy-start.7

commit v6 on v5

--- a/solution.py
+++ b/solution.py
@@ -50,17 +50,21 @@
     return jnp.where(head < HEADS_PLANE - 1, head % 2 * 4 + 8 * copy + head, 10 * copy + 4)
 
 
-def lean_of(head):
-    return jnp.where(head < HEADS_PLANE - 1, 0, 3)
+def odd_rows(head):
+    return jnp.where(head < HEADS_PLANE - 1, head % 2, 1)
 
 
 def asks(head, chip):
-    turned = (chip // 4 + lean_of(head)) % 4
-    return turned // 2, turned % 2 * 4 + chip % 4
+    x, y = chip % 4, chip // 4
+    own = y % 2 == odd_rows(head)
+    row = jnp.where(own, y, (y + 5 - 2 * ((x + head) % 2)) % 4)
+    return row // 2, jnp.where(own, x, 4 + x)
 
 
 def asked_by(head, copy, group):
-    return (2 * copy + group // 4 + 4 - lean_of(head)) % 4 * 4 + group % 4
+    x, row = group % 4, odd_rows(head) + 2 * copy
+    y = jnp.where(group < 4, row, (row + 3 + 2 * ((x + head) % 2)) % 4)
+    return y * 4 + x
 
 
 def device_of(plane, chip, core):

time: 211 us -> 204 us (0.967)
  Pallas kernels: 199 us -> 193 us
    pallas_call x1, Pallas kernels: 80.9 us -> 74.1 us  [home(): pl.pallas_call(home_kernel, name='home', out_shape=(out_shape,) * 3, in_s...]
where the time goes in v6:
time: 204 us; the launch traced here: 203 us
  Pallas kernels  193 us (95%)
  local copies, waits for them, and re-layouts  9.65 us (5%)
    pallas_call x1, Pallas kernels, bring(): pl.pallas_call(bring_kernel, name='bring', out_shape=(keys_shape, keys_sh...  80.8 us
    pallas_call x1, Pallas kernels, home(): pl.pallas_call(home_kernel, name='home', out_shape=(out_shape,) * 3, in_s...  74.1 us
    pallas_call x1, Pallas kernels, attend(): pl.pallas_call(attend_kernel, name='attend', out_shape=(query_shape, keys...  37.7 us
    unnamed x19, local copies, waits for them, and re-layouts  9.65 us

profile of v6, /device:TPU:1, one launch (start us, length us, event | category | flops | bytes accessed | tf_op | source)
XLA Modules:
  0.0 203.0 jit_solution(5756663112064055811)
XLA Ops:
  0.6 0.0 copy-start
  0.6 1.1 copy-done
  1.7 0.0 copy-start.1
  1.7 1.1 copy-done.1
  2.8 0.0 copy-start.2
  2.8 1.1 copy-done.2
  3.9 0.0 copy-start.3
  3.9 1.1 copy-done.3
  5.0 0.0 copy-start.5
  5.0 0.7 copy-done.5
  5.7 0.0 copy-start.6
  5.7 0.7 copy-done.6
  6.4 80.8 %bring.1 = (bf16[32,8,64,128]{3,2,1,0:T(8,128)(2,1)S(1)}, bf16[32,8,64,128]{3,2,1,0:T(8,128)(2,1)S(1)}, bf16[8,8,64,128]{3,2,1,0:T(8,128)(2,1)S(1)}, bf16[8,8,64...) custom-call(bf16[64,5120]{1,0:T(8,128)(2,1)S(1)} %copy-done, bf16[64,5120]{1,0:T(8,128)(2,1)S(1)} %copy-done.1, ...), custom_call_target="tpu_custom_call" | custom-call | tf_op jit(solution)/shard_map/bring/pallas_call | solution.py:297
  87.2 0.0 copy-start.4
  87.2 0.7 copy-done.4
  87.9 0.0 copy-start.7
  87.9 0.7 copy-done.7
  88.6 37.7 %attend.1 = (bf16[64,64,128]{2,1,0:T(8,128)(2,1)S(1)}, bf16[256,64,128]{2,1,0:T(8,128)(2,1)S(1)}, bf16[256,64,128]{2,1,0:T(8,128)(2,1)S(1)}) custom-call(s32[256]{0:T(256)S(1)} %copy-done.7, s32[16,256]{1,0:T(8,128)S(1)} %bitcast.19, bf16[64,64,128]{2,1,0:T(8,128)(2,1)S(1)} %bitcast.16, bf16[64,64,128]{2,1,0:T(8,128)(2,1)S(1)} %bitcast.17, ...), custom_call_target="tpu_custom_call" | custom-call | tf_op jit(solution)/shard_map/attend/pallas_call | solution.py:488
  126.3 74.1 %home.1 = (bf16[64,5120]{1,0:T(8,128)(2,1)S(1)}, bf16[64,5120]{1,0:T(8,128)(2,1)S(1)}, bf16[64,5120]{1,0:T(8,128)(2,1)S(1)}) custom-call(bf16[8,8,64,128]{3,2,1,0:T(8,128)(2,1)S(1)} %bitcast.15, bf16[32,8,64,128]{3,2,1,0:T(8,128)(2,1)S(1)} %bitcast.11, bf16[32,8,64,128]{3,2,1,0:T(8,128)(2,1)S(1)} %bitcast.12), custom_call_target="tpu_custom_call" | custom-call | tf_op jit(solution)/shard_map/home/pallas_call | solution.py:671
  200.5 0.8 copy.14
  201.3 0.8 copy.15
  202.1 0.8 copy.16
Async XLA Ops:
  0.6 1.1 copy-start
  1.7 1.1 copy-start.1
  2.8 1.1 copy-start.2
  3.9 1.1 copy-start.3
  5.0 0.7 copy-start.5
  5.7 0.7 copy-start.6
  87.2 0.7 copy-start.4
  87.9 0.7 copy-start.7

commit v7 on v6

--- a/solution.py
+++ b/solution.py
@@ -22,6 +22,7 @@
 WIDTH = HEADS_PLANE * HDIM
 QGROUPS = 8
 TOPK = 16
+SPAN = 16
 SLOTS = 2 * CHIPS * PLANES
 UNITS = QGROUPS * PLANES
 HALF = CUBE // 2
@@ -408,7 +409,10 @@
 
     def beside(ref, lists, c):
         return jnp.concatenate(
-            [jnp.concatenate([ref[s] for s in slots[c * 4:c * 4 + 4]], axis=0) for slots in lists],
+            [
+                jnp.concatenate([ref[s] for s in slots[c * SPAN:(c + 1) * SPAN]], axis=0)
+                for slots in lists
+            ],
             axis=1,
         )
 
@@ -428,12 +432,12 @@
             prob_old, dsc_old, wide_old = sides[old]
             lists_old = [[held[old, i * TOPK + r] for r in range(TOPK)] for i in range(2)]
             dquery = jnp.zeros((2 * CUBE, 2 * HDIM), F32)
-        for c in range(4):
+        for c in range(TOPK // SPAN):
             score.append(nt(beside(k, lists_new, c), wide_new[0]))
             dprob.append(nt(beside(v, lists_new, c), wide_new[1]))
             if old is None:
                 continue
-            chunk = slice(c * 4 * CUBE, (c + 1) * 4 * CUBE)
+            chunk = slice(c * SPAN * CUBE, (c + 1) * SPAN * CUBE)
             dscore = dsc_old[chunk]
             dquery += tn(dscore, beside(k, lists_old, c))
             key_terms = nn(dscore, wide_old[0])
@@ -441,17 +445,20 @@
             for i, slots in enumerate(lists_old):
                 lanes = slice(i * HDIM, (i + 1) * HDIM)
                 for total_of, terms in ((ak, key_terms), (av, value_terms)):
-                    before = [total_of[s] for s in slots[c * 4:c * 4 + 4]]
-                    for at, s in enumerate(slots[c * 4:c * 4 + 4]):
-                        total_of[s] = before[at] + terms[at * CUBE:(at + 1) * CUBE, lanes]
+                    for first in range(0, SPAN, 4):
+                        some = slots[c * SPAN + first:c * SPAN + first + 4]
+                        before = [total_of[s] for s in some]
+                        for at, s in enumerate(some):
+                            rows = slice((first + at) * CUBE, (first + at + 1) * CUBE)
+                            total_of[s] = before[at] + terms[rows, lanes]
         top = jnp.max(functools.reduce(jnp.maximum, score), axis=0, keepdims=True)
         weight = [jnp.exp2((s - top) * (factor * log2e)) for s in score]
         total = jnp.sum(functools.reduce(jnp.add, weight), axis=0, keepdims=True)
         inverse = 1.0 / total
         mixed = functools.reduce(jnp.add, [w * d for w, d in zip(weight, dprob)])
         center = jnp.sum(mixed, axis=0, keepdims=True) * inverse
-        for c in range(4):
-            chunk = slice(c * 4 * CUBE, (c + 1) * 4 * CUBE)
+        for c in range(TOPK // SPAN):
+            chunk = slice(c * SPAN * CUBE, (c + 1) * SPAN * CUBE)
             prob = weight[c] * inverse
             prob_new[chunk] = prob.astype(BF16)
             dsc_new[chunk] = (prob * (dprob[c] - center)).astype(BF16)

time: 204 us -> 204 us (level)
  no operation moved by 1% of the time
where the time goes in v7:
time: 204 us; the launch traced here: 203 us
  Pallas kernels  193 us (95%)
  local copies, waits for them, and re-layouts  9.65 us (5%)
    pallas_call x1, Pallas kernels, bring(): pl.pallas_call(bring_kernel, name='bring', out_shape=(keys_shape, keys_sh...  80.8 us
    pallas_call x1, Pallas kernels, home(): pl.pallas_call(home_kernel, name='home', out_shape=(out_shape,) * 3, in_s...  74.1 us
    pallas_call x1, Pallas kernels, attend(): pl.pallas_call(attend_kernel, name='attend', out_shape=(query_shape, keys...  38.1 us
    unnamed x19, local copies, waits for them, and re-layouts  9.65 us

profile of v7, /device:TPU:1, one launch (start us, length us, event | category | flops | bytes accessed | tf_op | source)
XLA Modules:
  0.0 203.2 jit_solution(917628257852209032)
XLA Ops:
  0.6 0.0 copy-start
  0.6 1.1 copy-done
  1.7 0.0 copy-start.1
  1.7 1.1 copy-done.1
  2.8 0.0 copy-start.2
  2.8 1.1 copy-done.2
  3.9 0.0 copy-start.3
  3.9 1.1 copy-done.3
  5.0 0.0 copy-start.5
  5.0 0.7 copy-done.5
  5.7 0.0 copy-start.6
  5.7 0.7 copy-done.6
  6.4 80.8 %bring.1 = (bf16[32,8,64,128]{3,2,1,0:T(8,128)(2,1)S(1)}, bf16[32,8,64,128]{3,2,1,0:T(8,128)(2,1)S(1)}, bf16[8,8,64,128]{3,2,1,0:T(8,128)(2,1)S(1)}, bf16[8,8,64...) custom-call(bf16[64,5120]{1,0:T(8,128)(2,1)S(1)} %copy-done, bf16[64,5120]{1,0:T(8,128)(2,1)S(1)} %copy-done.1, ...), custom_call_target="tpu_custom_call" | custom-call | tf_op jit(solution)/shard_map/bring/pallas_call | solution.py:298
  87.2 0.0 copy-start.4
  87.2 0.7 copy-done.4
  87.9 0.0 copy-start.7
  87.9 0.7 copy-done.7
  88.6 38.1 %attend.1 = (bf16[64,64,128]{2,1,0:T(8,128)(2,1)S(1)}, bf16[256,64,128]{2,1,0:T(8,128)(2,1)S(1)}, bf16[256,64,128]{2,1,0:T(8,128)(2,1)S(1)}) custom-call(s32[256]{0:T(256)S(1)} %copy-done.7, s32[16,256]{1,0:T(8,128)S(1)} %bitcast.19, bf16[64,64,128]{2,1,0:T(8,128)(2,1)S(1)} %bitcast.16, bf16[64,64,128]{2,1,0:T(8,128)(2,1)S(1)} %bitcast.17, ...), custom_call_target="tpu_custom_call" | custom-call | tf_op jit(solution)/shard_map/attend/pallas_call | solution.py:495
  126.6 74.1 %home.1 = (bf16[64,5120]{1,0:T(8,128)(2,1)S(1)}, bf16[64,5120]{1,0:T(8,128)(2,1)S(1)}, bf16[64,5120]{1,0:T(8,128)(2,1)S(1)}) custom-call(bf16[8,8,64,128]{3,2,1,0:T(8,128)(2,1)S(1)} %bitcast.15, bf16[32,8,64,128]{3,2,1,0:T(8,128)(2,1)S(1)} %bitcast.11, bf16[32,8,64,128]{3,2,1,0:T(8,128)(2,1)S(1)} %bitcast.12), custom_call_target="tpu_custom_call" | custom-call | tf_op jit(solution)/shard_map/home/pallas_call | solution.py:678
  200.7 0.8 copy.14
  201.6 0.8 copy.15
  202.4 0.8 copy.16
Async XLA Ops:
  0.6 1.1 copy-start
  1.7 1.1 copy-start.1
  2.8 1.1 copy-start.2
  3.9 1.1 copy-start.3
  5.0 0.7 copy-start.5
  5.7 0.7 copy-start.6
  87.2 0.7 copy-start.4
  87.9 0.7 copy-start.7

commit v8 on v6

--- a/solution.py
+++ b/solution.py
@@ -226,13 +226,29 @@
 
         lax.fori_loop(0, HEADS_PLANE, step, 0)
 
+    sibling = device_of(plane, chip, 1 - core)
+
+    def forward(number):
+        out = outs[number]
+
+        def step(d, _):
+            origin = (chip + CHIPS - d) % CHIPS
+            block = out.at[core * CHIPS + origin]
+            take_bytes(block, krecv.at[number, origin])
+            remote(block, block, fsend.at[number], frecv.at[number], sibling).start()
+            return 0
+
+        @pl.when(works)
+        def _():
+            lax.fori_loop(0, CHIPS, step, 0)
+
     for stage in range(STAGES):
         number, rows = stage // 2, rows_of(stage % 2)
         take_bytes(slabs[number].at[:, :, rows], zrecv.at[stage])
+        if stage + 2 == STAGES - 2:
+            start_along_z(STAGES, lambda t: pg.at[t], lambda t: pz.at[t])
         if stage + 2 < STAGES:
             start_stage(stage + 2)
-        if stage + 2 == STAGES:
-            start_along_z(STAGES, lambda t: pg.at[t], lambda t: pz.at[t])
         if number < 2:
             share_keys(number, rows)
         else:
@@ -241,23 +257,14 @@
                 lambda j, number=number, rows=rows: slabs[number].at[j, :, rows],
                 lambda i, number=number, rows=rows: outs[number].at[i, :, rows],
             )
-    take_bytes(pz, zrecv.at[STAGES])
-    share_queries(4, lambda j: pz, lambda i: ph.at[i])
-
-    sibling = device_of(plane, chip, 1 - core)
+        if stage == STAGES - 2:
+            take_bytes(pz, zrecv.at[STAGES])
+            share_queries(4, lambda j: pz, lambda i: ph.at[i])
+            forward(0)
+    forward(1)
 
     @pl.when(works)
     def _():
-        for number, out in ((0, kh), (1, vh)):
-            def forward(d, _, number=number, out=out):
-                origin = (chip + CHIPS - d) % CHIPS
-                block = out.at[core * CHIPS + origin]
-                take_bytes(block, krecv.at[number, origin])
-                remote(block, block, fsend.at[number], frecv.at[number], sibling).start()
-                return 0
-
-            lax.fori_loop(0, CHIPS, forward, 0)
-
         for number, out in enumerate((qh, fh, ph)):
             take_bytes(out, qrecv.at[number])
 
@@ -339,7 +346,6 @@
     works, head, copy = role_of(chip)
     units = jnp.where(works, UNITS, 0)
     factor = 1.0 / math.sqrt(HDIM)
-    log2e = math.log2(math.e)
 
     def eighths(source, group):
         block = source[pl.ds(pl.multiple_of(group * 8, 8), 8)].astype(F32)
@@ -445,7 +451,7 @@
                     for at, s in enumerate(slots[c * 4:c * 4 + 4]):
                         total_of[s] = before[at] + terms[at * CUBE:(at + 1) * CUBE, lanes]
         top = jnp.max(functools.reduce(jnp.maximum, score), axis=0, keepdims=True)
-        weight = [jnp.exp2((s - top) * (factor * log2e)) for s in score]
+        weight = [jnp.exp((s - top) * factor) for s in score]
         total = jnp.sum(functools.reduce(jnp.add, weight), axis=0, keepdims=True)
         inverse = 1.0 / total
         mixed = functools.reduce(jnp.add, [w * d for w, d in zip(weight, dprob)])

time: 204 us -> 205 us (level)
  no operation moved by 1% of the time
where the time goes in v8:
time: 205 us
  Pallas kernels  194 us (95%)
  local copies, waits for them, and re-layouts  9.65 us (5%)
    pallas_call x1, Pallas kernels, bring(): pl.pallas_call(bring_kernel, name='bring', out_shape=(keys_shape, keys_sh...  80.3 us
    pallas_call x1, Pallas kernels, home(): pl.pallas_call(home_kernel, name='home', out_shape=(out_shape,) * 3, in_s...  75.7 us
    pallas_call x1, Pallas kernels, attend(): pl.pallas_call(attend_kernel, name='attend', out_shape=(query_shape, keys...  38.4 us
    unnamed x19, local copies, waits for them, and re-layouts  9.65 us

profile of v8, /device:TPU:1, one launch (start us, length us, event | category | flops | bytes accessed | tf_op | source)
XLA Modules:
  0.0 204.7 jit_solution(17777257639295762141)
XLA Ops:
  0.6 0.0 copy-start
  0.6 1.1 copy-done
  1.7 0.0 copy-start.1
  1.7 1.1 copy-done.1
  2.8 0.0 copy-start.2
  2.8 1.1 copy-done.2
  3.9 0.0 copy-start.3
  3.9 1.1 copy-done.3
  5.0 0.0 copy-start.5
  5.0 0.7 copy-done.5
  5.7 0.0 copy-start.6
  5.7 0.7 copy-done.6
  6.4 80.3 %bring.1 = (bf16[32,8,64,128]{3,2,1,0:T(8,128)(2,1)S(1)}, bf16[32,8,64,128]{3,2,1,0:T(8,128)(2,1)S(1)}, bf16[8,8,64,128]{3,2,1,0:T(8,128)(2,1)S(1)}, bf16[8,8,64...) custom-call(bf16[64,5120]{1,0:T(8,128)(2,1)S(1)} %copy-done, bf16[64,5120]{1,0:T(8,128)(2,1)S(1)} %copy-done.1, ...), custom_call_target="tpu_custom_call" | custom-call | tf_op jit(solution)/shard_map/bring/pallas_call | solution.py:304
  86.7 0.0 copy-start.4
  86.7 0.7 copy-done.4
  87.4 0.0 copy-start.7
  87.4 0.7 copy-done.7
  88.1 38.4 %attend.1 = (bf16[64,64,128]{2,1,0:T(8,128)(2,1)S(1)}, bf16[256,64,128]{2,1,0:T(8,128)(2,1)S(1)}, bf16[256,64,128]{2,1,0:T(8,128)(2,1)S(1)}) custom-call(s32[256]{0:T(256)S(1)} %copy-done.7, s32[16,256]{1,0:T(8,128)S(1)} %bitcast.19, bf16[64,64,128]{2,1,0:T(8,128)(2,1)S(1)} %bitcast.16, bf16[64,64,128]{2,1,0:T(8,128)(2,1)S(1)} %bitcast.17, ...), custom_call_target="tpu_custom_call" | custom-call | tf_op jit(solution)/shard_map/attend/pallas_call | solution.py:494
  126.5 75.7 %home.1 = (bf16[64,5120]{1,0:T(8,128)(2,1)S(1)}, bf16[64,5120]{1,0:T(8,128)(2,1)S(1)}, bf16[64,5120]{1,0:T(8,128)(2,1)S(1)}) custom-call(bf16[8,8,64,128]{3,2,1,0:T(8,128)(2,1)S(1)} %bitcast.15, bf16[32,8,64,128]{3,2,1,0:T(8,128)(2,1)S(1)} %bitcast.11, bf16[32,8,64,128]{3,2,1,0:T(8,128)(2,1)S(1)} %bitcast.12), custom_call_target="tpu_custom_call" | custom-call | tf_op jit(solution)/shard_map/home/pallas_call | solution.py:677
  202.2 0.8 copy.14
  203.1 0.8 copy.15
  203.9 0.8 copy.16
Async XLA Ops:
  0.6 1.1 copy-start
  1.7 1.1 copy-start.1
  2.8 1.1 copy-start.2
  3.9 1.1 copy-start.3
  5.0 0.7 copy-start.5
  5.7 0.7 copy-start.6
  86.7 0.7 copy-start.4
  87.4 0.7 copy-start.7

commit v9 on v8

--- a/solution.py
+++ b/solution.py
@@ -113,7 +113,7 @@
 
 
 def bring_kernel(
-    k_in, v_in, q_in, g_in, fgate, cgate,
+    tokens, gates_in,
     kh, vh, qh, fh, ph,
     packed, kz, vz, qz, fz, pz, pg,
     zsend, zrecv, psend, krecv, qrecv, fsend, frecv,
@@ -144,28 +144,30 @@
             lambda t: slabs[number].at[:, t, rows],
         )
 
-    def pack(number, source):
+    def pack(number):
         def step(group, _):
             for j in range(HEADS_PLANE):
-                packed[number, group, j] = source[:, columns(group * HEADS_PLANE + j, HDIM)]
+                packed[number, group, j] = tokens[number, :, columns(group * HEADS_PLANE + j, HDIM)]
             return 0
 
         lax.fori_loop(0, PLANES, step, 0)
 
-    pack(0, k_in)
+    pack(0)
     start_stage(0)
-    pack(1, v_in)
-    pack(2, q_in)
+    pack(1)
+    pack(2)
+
+    heads = gates_in.shape[0] // 2
 
     def gates(group, _):
-        row = lax.broadcasted_iota(jnp.int32, (fgate.shape[0], WIDTH), 0)
-        col = lax.broadcasted_iota(jnp.int32, (fgate.shape[0], WIDTH), 1)
+        row = lax.broadcasted_iota(jnp.int32, (heads, WIDTH), 0)
+        col = lax.broadcasted_iota(jnp.int32, (heads, WIDTH), 1)
         spread = jnp.where(
             row == group * HEADS_PLANE + lax.shift_right_logical(col, 7), 1.0, 0.0
         ).astype(BF16)
-        grad = g_in[:, columns(group)].astype(F32)
-        fine = (tn(fgate[...], spread) * grad).astype(BF16)
-        coarse = tn(cgate[...], spread)
+        grad = tokens[3, :, columns(group)].astype(F32)
+        fine = (tn(gates_in[:heads], spread) * grad).astype(BF16)
+        coarse = tn(gates_in[heads:], spread)
         pooled = jnp.sum(coarse * grad, axis=0, keepdims=True)
         rows = []
         for j in range(HEADS_PLANE):
@@ -305,7 +307,7 @@
         bring_kernel,
         name="bring",
         out_shape=(keys_shape, keys_shape, query_shape, query_shape, pooled_shape),
-        in_specs=[in_vmem] * 6,
+        in_specs=[in_vmem] * 2,
         out_specs=[anywhere] * 5,
         scratch_shapes=[
             pltpu.VMEM((4, PLANES, HEADS_PLANE, CUBE, HDIM), BF16),
@@ -321,7 +323,10 @@
         compiler_params=pltpu.CompilerParams(
             collective_id=0, has_side_effects=True, vmem_limit_bytes=BRING_VMEM
         ),
-    )(keys_in, values, queries, grad_out, fine_gate.T, coarse_gate.T)
+    )(
+        jnp.stack([keys_in, values, queries, grad_out]),
+        jnp.concatenate([fine_gate.T, coarse_gate.T], axis=0),
+    )
 
 
 def nt(a, b):
@@ -346,6 +351,7 @@
     works, head, copy = role_of(chip)
     units = jnp.where(works, UNITS, 0)
     factor = 1.0 / math.sqrt(HDIM)
+    log2e = math.log2(math.e)
 
     def eighths(source, group):
         block = source[pl.ds(pl.multiple_of(group * 8, 8), 8)].astype(F32)
@@ -451,7 +457,7 @@
                     for at, s in enumerate(slots[c * 4:c * 4 + 4]):
                         total_of[s] = before[at] + terms[at * CUBE:(at + 1) * CUBE, lanes]
         top = jnp.max(functools.reduce(jnp.maximum, score), axis=0, keepdims=True)
-        weight = [jnp.exp((s - top) * factor) for s in score]
+        weight = [jnp.exp2((s - top) * (factor * log2e)) for s in score]
         total = jnp.sum(functools.reduce(jnp.add, weight), axis=0, keepdims=True)
         inverse = 1.0 / total
         mixed = functools.reduce(jnp.add, [w * d for w, d in zip(weight, dprob)])

time: 205 us -> 200 us (0.976)
  local copies, waits for them, and re-layouts: 9.65 us -> 2.52 us
  other arithmetic: 0 us -> 2.73 us
    unnamed x19 -> x7, local copies, waits for them, and re-layouts: 9.65 us -> 2.52 us
    pallas_call x1, Pallas kernels: 75.7 us -> 72.7 us  [home(): pl.pallas_call(home_kernel, name='home', out_shape=(out_shape,) * 3, in_s...]
where the time goes in v9:
time: 200 us; the launch traced here: 198 us
  Pallas kernels  192 us (96%)
  other arithmetic  2.73 us (1%)
  local copies, waits for them, and re-layouts  2.52 us (1%)
    pallas_call x1, Pallas kernels, bring(): pl.pallas_call(bring_kernel, name='bring', out_shape=(keys_shape, keys_sh...  81 us
    pallas_call x1, Pallas kernels, home(): pl.pallas_call(home_kernel, name='home', out_shape=(out_shape,) * 3, in_s...  72.7 us
    pallas_call x1, Pallas kernels, attend(): pl.pallas_call(attend_kernel, name='attend', out_shape=(query_shape, keys...  38.5 us

profile of v9, /device:TPU:1, one launch (start us, length us, event | category | flops | bytes accessed | tf_op | source)
XLA Modules:
  0.0 198.2 jit_solution(4784502108406608237)
XLA Ops:
  0.6 0.7 pad_maximum_fusion.1.gates_in
  1.4 2.0 %pad_maximum_fusion.tokens = bf16[4,64,5120]{2,1,0:T(8,128)(2,1)S(1)} fusion(bf16[1,64,5120]{2,1,0:T(8,128)(2,1)} %bitcast.24, bf16[1,64,5120]{2,1,0:T(8,128)(2,1)} %bitcast.25, bf16[1,64,5120]{2,1,0:T(8,128)(2,1)} %bitcast.26, bf16[1,64,5120]{2,1,0:T(8,128)(2,1)} %bitcast.27), kind=kLoop, calls=%fused_computation | loop fusion | flops 3932160 | bytes 5242880 | tf_op jit(solution)/shard_map/stack | solution.py:327
  3.4 0.0 copy-start
  3.4 0.0 copy-start.1
  3.4 81.0 %bring.1 = (bf16[32,8,64,128]{3,2,1,0:T(8,128)(2,1)S(1)}, bf16[32,8,64,128]{3,2,1,0:T(8,128)(2,1)S(1)}, bf16[8,8,64,128]{3,2,1,0:T(8,128)(2,1)S(1)}, bf16[8,8,64...) custom-call(bf16[4,64,5120]{2,1,0:T(8,128)(2,1)S(1)} %pad_maximum_fusion.tokens, ...), custom_call_target="tpu_custom_call" | custom-call | tf_op jit(solution)/shard_map/bring/pallas_call | solution.py:306
  84.4 0.0 copy-done
  84.4 0.0 copy-done.1
  84.4 38.5 %attend.1 = (bf16[64,64,128]{2,1,0:T(8,128)(2,1)S(1)}, bf16[256,64,128]{2,1,0:T(8,128)(2,1)S(1)}, bf16[256,64,128]{2,1,0:T(8,128)(2,1)S(1)}) custom-call(s32[256]{0:T(256)S(1)} %copy-done.1, s32[16,256]{1,0:T(8,128)S(1)} %bitcast.23, bf16[64,64,128]{2,1,0:T(8,128)(2,1)S(1)} %bitcast.20, bf16[64,64,128]{2,1,0:T(8,128)(2,1)S(1)} %bitcast.21, ...), custom_call_target="tpu_custom_call" | custom-call | tf_op jit(solution)/shard_map/attend/pallas_call | solution.py:500
  122.9 72.7 %home.1 = (bf16[64,5120]{1,0:T(8,128)(2,1)S(1)}, bf16[64,5120]{1,0:T(8,128)(2,1)S(1)}, bf16[64,5120]{1,0:T(8,128)(2,1)S(1)}) custom-call(bf16[8,8,64,128]{3,2,1,0:T(8,128)(2,1)S(1)} %bitcast.19, bf16[32,8,64,128]{3,2,1,0:T(8,128)(2,1)S(1)} %bitcast.15, bf16[32,8,64,128]{3,2,1,0:T(8,128)(2,1)S(1)} %bitcast.16), custom_call_target="tpu_custom_call" | custom-call | tf_op jit(solution)/shard_map/home/pallas_call | solution.py:683
  195.7 0.8 copy.14
  196.5 0.8 copy.15
  197.3 0.8 copy.16
Async XLA Ops:
  3.4 81.0 %copy-start = (s32[256,16]{0,1:T(8,128)S(1)}, s32[256,16]{0,1:T(8,128)}, u32[]{:S(2)}) copy-start(s32[256,16]{0,1:T(8,128)} %param.15) | copy-start | bytes 49156
  3.4 81.0 %copy-start.1 = (s32[256]{0:T(256)S(1)}, s32[256]{0:T(256)}, u32[]{:S(2)}) copy-start(s32[256]{0:T(256)} %toc.1) | copy-start | bytes 3076

commit v10 on v9

--- a/solution.py
+++ b/solution.py
@@ -532,7 +532,7 @@
 
 def home_kernel(
     dq, dk, dv,
-    oq, ok, ov,
+    grads,
     own_k, own_v, sib_k, sib_v, land_q, land_k, land_v, sum_k, sum_v, sum_q,
     ssend, srecv, psend, precv, zsend, zrecv,
 ):
@@ -540,6 +540,7 @@
     works, head, replica = role_of(chip)
     greet(plane, chip, core)
     sibling = device_of(plane, chip, 1 - core)
+    oq, ok, ov = grads.at[0], grads.at[1], grads.at[2]
     sources, owns, sibs = (dk, dv), (own_k, own_v), (sib_k, sib_v)
     lands, sums, outs = (land_k, land_v), (sum_k, sum_v), (ok, ov)
     mine = columns(plane)
@@ -675,7 +676,7 @@
 def home(dq, dk, dv, rows, width):
     anywhere = pl.BlockSpec(memory_space=pl.ANY)
     in_vmem = pl.BlockSpec(memory_space=pltpu.VMEM)
-    out_shape = jax.ShapeDtypeStruct((rows, width), BF16)
+    out_shape = jax.ShapeDtypeStruct((3, rows, width), BF16)
     half = pltpu.VMEM((CHIPS, PLANES, CUBE, HDIM), BF16)
     slab = pltpu.VMEM((PLANES, CUBE, WIDTH), BF16)
     by_head = pltpu.VMEM((HEADS_PLANE, PLANES, CUBE, HDIM), BF16)
@@ -683,9 +684,9 @@
     return pl.pallas_call(
         home_kernel,
         name="home",
-        out_shape=(out_shape,) * 3,
+        out_shape=out_shape,
         in_specs=[anywhere, in_vmem, in_vmem],
-        out_specs=[anywhere] * 3,
+        out_specs=anywhere,
         scratch_shapes=[
             half, half, half, half, by_head, copies, copies, slab, slab, slab,
             pltpu.SemaphoreType.DMA((2,)),
@@ -708,7 +709,8 @@
 def on_device(queries, keys_in, values, grad_out, fine_gate, coarse_gate, tile_of_cube, select):
     kh, vh, qh, fh, ph = bring(keys_in, values, queries, grad_out, fine_gate, coarse_gate)
     dq, dk, dv = attend(tile_of_cube, select, qh, fh, ph, kh, vh)
-    return home(dq, dk, dv, *queries.shape)
+    grads = home(dq, dk, dv, *queries.shape)
+    return grads[0], grads[1], grads[2]
 
 
 def solution(mesh):

time: 200 us -> 199 us (level)
    unnamed x7 -> x4, local copies, waits for them, and re-layouts: 2.52 us -> 0.01 us
where the time goes in v10:
time: 199 us; the launch traced here: 197 us
  Pallas kernels  192 us (96%)
  other arithmetic  2.73 us (1%)
    pallas_call x1, Pallas kernels, bring(): pl.pallas_call(bring_kernel, name='bring', out_shape=(keys_shape, keys_sh...  81 us
    pallas_call x1, Pallas kernels, home(): pl.pallas_call(home_kernel, name='home', out_shape=out_shape, in_specs=[a...  72.7 us
    pallas_call x1, Pallas kernels, attend(): pl.pallas_call(attend_kernel, name='attend', out_shape=(query_shape, keys...  38.5 us

profile of v10, /device:TPU:1, one launch (start us, length us, event | category | flops | bytes accessed | tf_op | source)
XLA Modules:
  0.0 196.9 jit_solution(15623956692919537476)
XLA Ops:
  0.6 0.7 pad_maximum_fusion.1.gates_in
  1.4 2.0 %pad_maximum_fusion.tokens = bf16[4,64,5120]{2,1,0:T(8,128)(2,1)S(1)} fusion(bf16[1,64,5120]{2,1,0:T(8,128)(2,1)} %bitcast.30, bf16[1,64,5120]{2,1,0:T(8,128)(2,1)} %bitcast.31, bf16[1,64,5120]{2,1,0:T(8,128)(2,1)} %bitcast.32, bf16[1,64,5120]{2,1,0:T(8,128)(2,1)} %bitcast.33), kind=kLoop, calls=%fused_computation | loop fusion | flops 3932160 | bytes 5242880 | tf_op jit(solution)/shard_map/stack | solution.py:327
  3.4 0.0 copy-start
  3.4 0.0 copy-start.1
  3.4 81.0 %bring.1 = (bf16[32,8,64,128]{3,2,1,0:T(8,128)(2,1)S(1)}, bf16[32,8,64,128]{3,2,1,0:T(8,128)(2,1)S(1)}, bf16[8,8,64,128]{3,2,1,0:T(8,128)(2,1)S(1)}, bf16[8,8,64...) custom-call(bf16[4,64,5120]{2,1,0:T(8,128)(2,1)S(1)} %pad_maximum_fusion.tokens, ...), custom_call_target="tpu_custom_call" | custom-call | tf_op jit(solution)/shard_map/bring/pallas_call | solution.py:306
  84.4 0.0 copy-done
  84.4 0.0 copy-done.1
  84.4 38.5 %attend.1 = (bf16[64,64,128]{2,1,0:T(8,128)(2,1)S(1)}, bf16[256,64,128]{2,1,0:T(8,128)(2,1)S(1)}, bf16[256,64,128]{2,1,0:T(8,128)(2,1)S(1)}) custom-call(s32[256]{0:T(256)S(1)} %copy-done.1, s32[16,256]{1,0:T(8,128)S(1)} %bitcast.29, bf16[64,64,128]{2,1,0:T(8,128)(2,1)S(1)} %bitcast.25, bf16[64,64,128]{2,1,0:T(8,128)(2,1)S(1)} %bitcast.26, ...), custom_call_target="tpu_custom_call" | custom-call | tf_op jit(solution)/shard_map/attend/pallas_call | solution.py:500
  122.9 72.7 %home.1 = bf16[3,64,5120]{2,1,0:T(8,128)(2,1)S(1)} custom-call(bf16[8,8,64,128]{3,2,1,0:T(8,128)(2,1)S(1)} %bitcast.27, bf16[32,8,64,128]{3,2,1,0:T(8,128)(2,1)S(1)} %bitcast.23, bf16[32,8,64,128]{3,2,1,0:T(8,128)(2,1)S(1)} %bitcast.24), custom_call_target="tpu_custom_call" | custom-call | tf_op jit(solution)/shard_map/home/pallas_call | solution.py:684
  195.6 1.3 slice_bitcast_fusion
Async XLA Ops:
  3.4 81.0 %copy-start = (s32[256,16]{0,1:T(8,128)S(1)}, s32[256,16]{0,1:T(8,128)}, u32[]{:S(2)}) copy-start(s32[256,16]{0,1:T(8,128)} %param.15) | copy-start | bytes 49156
  3.4 81.0 %copy-start.1 = (s32[256]{0:T(256)S(1)}, s32[256]{0:T(256)}, u32[]{:S(2)}) copy-start(s32[256]{0:T(256)} %toc.1) | copy-start | bytes 3076
